TPU v7x, 768 devices: a whole 4x8x12 slice. The times are simulated.
768 devices in a mesh: dp: 12 (over z), tensor: 8 (over y), pipe: 8 (over x, core).
Axes of the slice: x: 4, y: 8, z: 12, core: 2. Of those that a mesh axis runs over, the one named last changes fastest.
Arguments:
- old_weight: float32 [36864, 4096], P(('dp', 'pipe'), 'tensor'), may hold values from -6 to 6
- old_first_moment: float32 [36864, 4096], P(('dp', 'pipe'), 'tensor'), may hold values from -1.8 to 1.8
- old_second_moment: float32 [36864, 4096], P(('dp', 'pipe'), 'tensor'), may hold values from 0.1 to 2
- gradient: bfloat16 [24576, 4096], P(('dp', 'pipe'), 'tensor'), may hold values from -6 to 6
- hidden: bfloat16 [24576, 3072], P(('dp', 'pipe')), may hold values from -0.15625 to 0.15625
- residual: bfloat16 [3072, 4096], P(('dp', 'pipe'), 'tensor'), may hold values from -64 to 64
- norm_gain: float32 [4096], P('tensor'), may hold values from 0.1 to 1.9
- old_starts: int32 [97], replicated, may hold values from 0 to 112, as said below
- new_starts: int32 [97], replicated, may hold values from 0 to 112, as said below
Outputs:
- new_weight: float32 [24576, 4096], P(('dp', 'pipe'), 'tensor')
- new_first_moment: float32 [24576, 4096], P(('dp', 'pipe'), 'tensor')
- new_second_moment: float32 [24576, 4096], P(('dp', 'pipe'), 'tensor')
- layer_out: bfloat16 [3072, 4096], P(('dp', 'pipe'), 'tensor')
Inputs may be any that keep to these rules, and one draw needn't show every extreme that they name: Data index d owns blocks new_starts[d] to new_starts[d+1] - 1, between 1 and 2 of them, and 2 for some index; new_starts begins at 0 and ends at 112. Block slots past a device's count in gradient and hidden are not part of the data. Data index d held blocks old_starts[d] to old_starts[d+1] - 1, at most 3 of them and 3 for some index; an index d with d % 4 == 3 held none, every other index at least one. The new owner of every block is its old holder or the next data index; the blocks that a holder hands to the next index are that index's first blocks, at most 2 of them, and 2 for some index. old_starts begins at 0 and ends at 112. Block slots past a holder's count are not part of the data.
All inputs are finite; a program needn't handle non-finite values.
Results may differ from a plain program's by a relative error of at most 0.0035.
Values sent between devices are 32-bit elements; how exact they have to be, the bound alone decides.
No kernel may reach another device: no remote copies, remote signals or barrier semaphores. Data moves between devices by JAX's collectives and lax.ppermute only.
A program may use at most 64 MiB of HBM per device.

v0:
```python
import jax
import jax.numpy as jnp
from jax import lax
from jax.sharding import PartitionSpec as P

D = 4096
BLOCK_ROWS = 128
STEP = 20


decay_first = 0.9
decay_second = 0.95
learn_rate = 0.05
weight_decay = 0.1
adam_eps = 1e-08
norm_eps = 1e-05


def from_behind(block, axis, distance):
    devices = range(lax.axis_size(axis))
    route = [(i - distance, i) for i in devices if i - distance in devices]
    return lax.ppermute(block, axis, route)


def select_blocks(source, slot_ids, live_mask, slot_total, block_rows):
    blocks = source.reshape(slot_total, block_rows, source.shape[1])
    chosen = jnp.take(blocks, slot_ids, axis=0)
    return jnp.where(live_mask[:, None, None], chosen, 0.0)


def on_device(
    old_weight,
    old_first_moment,
    old_second_moment,
    gradient,
    hidden,
    residual,
    norm_gain,
    old_starts,
    new_starts,
):
    block_rows = BLOCK_ROWS
    columns = old_weight.shape[1]
    old_total = old_weight.shape[0] // block_rows
    new_total = gradient.shape[0] // block_rows
    position = lax.axis_index(("dp", "pipe"))
    old_head = old_starts[position]
    old_tail = old_starts[position + 1]
    new_head = new_starts[position]
    new_tail = new_starts[position + 1]
    lane_ids = jnp.arange(new_total, dtype=jnp.int32)
    send_slots = jnp.clip(new_tail + lane_ids - old_head, 0, old_total - 1)
    send_mask = lane_ids < old_tail - new_tail
    keep_slots = jnp.clip(new_head + lane_ids - old_head, 0, old_total - 1)
    live_mask = lane_ids < new_tail - new_head
    arrived = lane_ids < jnp.minimum(old_head, new_tail) - new_head
    sources = (old_weight, old_first_moment, old_second_moment)
    outgoing = jnp.stack(
        [select_blocks(source, send_slots, send_mask, old_total, block_rows) for source in sources]
    )
    kept = jnp.stack(
        [select_blocks(source, keep_slots, live_mask, old_total, block_rows) for source in sources]
    )
    incoming = from_behind(outgoing, ("dp", "pipe"), 1)
    state = jnp.where(arrived[None, :, None, None], incoming, kept)
    weight_old = state[0]
    first_old = state[1]
    second_old = state[2]
    gradient_f = gradient.reshape(new_total, block_rows, columns).astype(jnp.float32)
    first_new = decay_first * first_old + (1.0 - decay_first) * gradient_f
    second_new = decay_second * second_old + (1.0 - decay_second) * gradient_f * gradient_f
    corr_first = 1.0 - decay_first**STEP
    corr_second = 1.0 - decay_second**STEP
    step_dir = first_new / corr_first / (jnp.sqrt(second_new / corr_second) + adam_eps)
    weight_next = weight_old - learn_rate * (step_dir + weight_decay * weight_old)
    live_blocks = live_mask[:, None, None]
    new_weight = jnp.where(live_blocks, weight_next, 0.0)
    new_first = jnp.where(live_blocks, first_new, 0.0)
    new_second = jnp.where(live_blocks, second_new, 0.0)
    weight_half = new_weight.astype(jnp.bfloat16).reshape(new_total * block_rows, columns)
    projection = lax.psum_scatter(
        lax.dot_general(
            hidden, weight_half, (((0,), (0,)), ((), ())), preferred_element_type=jnp.float32
        ),
        ("dp", "pipe"),
        scatter_dimension=0,
        tiled=True,
    )
    summed = residual.astype(jnp.float32) + projection
    row_total = lax.psum(jnp.sum(summed * summed, axis=1), "tensor")
    row_scale = lax.rsqrt(row_total / D + norm_eps)
    layer_out = (summed * row_scale[:, None] * norm_gain[None, :]).astype(jnp.bfloat16)
    return (
        new_weight.reshape(new_total * block_rows, columns),
        new_first.reshape(new_total * block_rows, columns),
        new_second.reshape(new_total * block_rows, columns),
        layer_out,
    )


def solution(mesh):
    return jax.shard_map(
        on_device,
        mesh=mesh,
        in_specs=(
            P(("dp", "pipe"), "tensor"),
            P(("dp", "pipe"), "tensor"),
            P(("dp", "pipe"), "tensor"),
            P(("dp", "pipe"), "tensor"),
            P(("dp", "pipe"), None),
            P(("dp", "pipe"), "tensor"),
            P("tensor"),
            P(),
            P(),
        ),
        out_specs=(
            P(("dp", "pipe"), "tensor"),
            P(("dp", "pipe"), "tensor"),
            P(("dp", "pipe"), "tensor"),
            P(("dp", "pipe"), "tensor"),
        ),
        check_vma=False,
    )
```

profile of v0, /device:TPU:6, one launch (start us, length us, event | category | flops | bytes accessed | tf_op | source)
XLA Modules:
  0.0 303.8 jit_solution(7000155511667921414)
XLA Ops:
  7.2 0.0 copy-start
  7.2 0.0 reduce-scatter.4.cloned.1.call-start
  7.2 1.4 fusion.14
  8.7 1.3 compare_and_fusion.1
  11.3 1.7 gather_fusion
  13.0 1.7 gather_fusion.1
  14.7 1.7 gather_fusion.2
  16.4 0.4 fusion.10
  16.8 0.0 copy-start.2
  16.8 1.3 pad_maximum_fusion
  18.1 1.9 collective-permute-start
  21.3 1.3 compare_and_fusion
  22.6 0.0 copy-done.2
  22.6 0.6 gather_fusion.3
  23.2 1.7 gather_fusion.4
  25.0 1.7 gather_fusion.5
  28.7 0.1 broadcast_bitcast_fusion
  28.7 0.3 fusion.7
  29.0 11.1 %collective-permute-done = f32[3,2,128,512]{3,2,1,0:T(8,128)} collective-permute-done((f32[3,2,128,512]{3,2,1,0:T(8,128)}, f32[3,2,128,512]{3,2,1,0:T(8,128)}, u32[]{:S(2)}, u32[]{:S(2)}) %collective-permute-start) | collective-permute-done | bytes 1572896 | tf_op jit(solution)/shard_map/ppermute | solution.py:22
  40.1 1.8 maximum_select_fusion
  42.0 0.0 copy-start.3
  42.0 0.2 slice_multiply_fusion
  42.2 0.7 copy-done.3
  42.9 1.5 fusion.12
  44.4 0.0 copy-start.1
  44.4 0.0 copy-done
  44.4 3.6 %convolution_bitcast_fusion = f32[3072,512]{0,1:T(8,128)} fusion(bf16[256,3072]{1,0:T(8,128)(2,1)S(1)} %copy-done, f32[256,512]{1,0:T(8,128)S(1)} %get-tuple-element.21), kind=kOutput, calls=%fused_computation.6 | convolution fusion | flops 805437440 | bytes 8388608 | tf_op jit(solution)/shard_map/dot_general | solution.py:82
  48.0 0.0 copy-done.1
  48.0 6.6 %copy.17 = f32[3072,512]{1,0:T(8,128)} copy(f32[3072,512]{0,1:T(8,128)} %convolution_bitcast_fusion) | data formatting | bytes 12582912
  54.6 0.0 copy-start.4
  54.6 0.0 copy-start.5
  54.6 0.0 reduce-scatter.4.cloned.1.call-update
  54.7 0.7 copy-done.4
  55.4 0.1 copy.15
  55.5 222.5 %reduce-scatter.4.cloned.1.call-done = f32[32,512]{1,0:T(8,128)} async-done(((f32[3072,512]{1,0:T(8,128)}), f32[32,512]{1,0:T(8,128)}) %reduce-scatter.4.cloned.1.call-update) | async-done | bytes 65552
  278.0 1.0 copy.18
  279.0 0.1 multiply_reduce_fusion
  279.1 17.0 %psum.7 = f32[32]{0:T(128)S(1)} all-reduce(f32[32]{0:T(128)S(1)} %multiply_reduce_fusion), channel_id=1, replica_groups=mesh['dp'=12,'tensor'=8,'pipe'=8] {'tensor'}, use_global_device_ids=true, to_apply=%region_2.4 | all-reduce | flops 32 | bytes 256 | tf_op jit(solution)/shard_map/psum | solution.py:90
  296.1 0.0 copy-done.5
  296.1 0.1 multiply_convert_fusion
  296.2 0.7 copy.16
  (6 shorter events, 0.0 us)
Async XLA Ops:
  7.2 37.2 %copy-start = (bf16[256,3072]{1,0:T(8,128)(2,1)S(1)}, bf16[256,3072]{1,0:T(8,128)(2,1)}, u32[]{:S(2)}) copy-start(bf16[256,3072]{1,0:T(8,128)(2,1)} %param.15) | copy-start | bytes 4718596
  7.2 270.8 %reduce-scatter.4.cloned.1.call-start = ((), (), s32[]{:S(2)}) async-start(), calls=%async_computation.1 | async-start | bytes 6356992
  16.8 5.8 %copy-start.2 = (f32[384,512]{1,0:T(8,128)S(1)}, f32[384,512]{1,0:T(8,128)}, u32[]{:S(2)}) copy-start(f32[384,512]{1,0:T(8,128)} %param.11) | copy-start | bytes 2359300
  18.1 22.0 %collective-permute-start = (f32[3,2,128,512]{3,2,1,0:T(8,128)}, f32[3,2,128,512]{3,2,1,0:T(8,128)}, u32[]{:S(2)}, u32[]{:S(2)}) collective-permute-start(f32[3,2,128,512]{3,2,1,0:T(8,128)} %pad_maximum_fusion), channel_id=1, source_target_pairs={{0,1},{1,2},{2,3},{3,4},{4,5},{5,6},{6,7},{7,64},{64,65},{65,66},{... | collective-permute-start | bytes 4718600 | tf_op jit(solution)/shard_map/ppermute | solution.py:22
  42.0 1.0 copy-start.3
  44.4 3.6 %copy-start.1 = (f32[256,512]{1,0:T(8,128)}, f32[256,512]{1,0:T(8,128)S(1)}, u32[]{:S(2)}) copy-start(f32[256,512]{1,0:T(8,128)S(1)} %get-tuple-element.21) | copy-start | bytes 1572868
  54.6 0.8 copy-start.4
  54.6 241.5 %copy-start.5 = (f32[512]{0:T(512)S(1)}, f32[512]{0:T(512)}, u32[]{:S(2)}) copy-start(f32[512]{0:T(512)} %param.17) | copy-start | bytes 6148
Sparse Core Ops, SparseCore 0:
  54.8 223.1 reduce-scatter.3
where the time goes:
time: 305 us; the launch traced here: 304 us
  waiting for transfers between devices  234 us (77%)
  local copies, waits for them, and re-layouts  20.5 us (7%)
  between operations  18.8 us (6%)
  blocking collectives  17 us (6%)
  other arithmetic  8.25 us (3%)
  matrix products  3.64 us (1%)
    unnamed x2, waiting for transfers between devices  223 us
    psum x1, blocking collectives, on_device(): row_total = lax.psum(jnp.sum(summed * summed, axis=1), 'tensor')  17 us
    ppermute x1, waiting for transfers between devices, from_behind(): return lax.ppermute(block, axis, route)  11.1 us
    unnamed x16, local copies, waits for them, and re-layouts  9.86 us
    gather x6, local copies, waits for them, and re-layouts, select_blocks(): chosen = jnp.take(blocks, slot_ids, axis=0)  9.16 us
  transfers between devices with their start and end apart: 2, of which 2 were waited for; matrix products, arithmetic and copies ran while one was open for 2% of the time, Pallas kernels for 0%

commit v1 on v0

v1 whole, which is shorter than its diff:
```python
import functools

import jax
import jax.numpy as jnp
from jax import lax
from jax.experimental import pallas as pl
from jax.experimental.pallas import tpu as pltpu
from jax.sharding import PartitionSpec as P

BLOCK_ROWS = 128
STEP = 20
SEAT = 32

decay_first = 0.9
decay_second = 0.95
learn_rate = 0.05
weight_decay = 0.1
adam_eps = 1e-08
norm_eps = 1e-05
corr_first = 1.0 - decay_first**STEP
corr_second = 1.0 - decay_second**STEP

DATA = ("dp", "pipe")
F32 = jnp.float32
BF16 = jnp.bfloat16
MIB = 1024 * 1024
COST = pl.CostEstimate(flops=0, bytes_accessed=1024, transcendentals=0)


def params(mib=32):
    return pltpu.CompilerParams(vmem_limit_bytes=mib * MIB)


def clip(value, low, high):
    return jnp.minimum(jnp.maximum(value, low), high)


def send_slot(pos, old_starts, new_starts):
    return clip(new_starts[pos + 1] - old_starts[pos], 0, 1)


def arrival_slot(lane, pos, old_starts, new_starts):
    before = jnp.maximum(pos - 1, 0)
    first = new_starts[pos] - old_starts[before]
    return clip(first - clip(first, 0, 1) + lane, 0, 1)


def kept_slot(lane, pos, old_starts, new_starts):
    return clip(new_starts[pos] + lane - old_starts[pos], 0, 2)


def take_kernel(pos, old_starts, new_starts, *refs):
    sources, out, held, arrivals, departures = refs[:3], *refs[3:]
    slot = send_slot(pos[0], old_starts, new_starts)
    into, onto = [], []
    for i, source in enumerate(sources):
        for lane in range(2):
            there = pl.multiple_of((slot + lane) * BLOCK_ROWS, BLOCK_ROWS)
            here = pl.ds(lane * BLOCK_ROWS, BLOCK_ROWS)
            into.append(
                pltpu.make_async_copy(
                    source.at[pl.ds(there, BLOCK_ROWS), :],
                    held.at[i, here, :],
                    arrivals.at[i, lane],
                )
            )
            onto.append(
                pltpu.make_async_copy(
                    held.at[i, here, :], out.at[i, here, :], departures.at[i, lane]
                )
            )
    for copy in into:
        copy.start()
    for copy, following in zip(into, onto):
        copy.wait()
        following.start()
    for copy in onto:
        copy.wait()


def take_moved(scalars, olds):
    shape = (3, 2 * BLOCK_ROWS, olds[0].shape[1])
    return pl.pallas_call(
        take_kernel,
        in_specs=[pl.BlockSpec(memory_space=pltpu.SMEM)] * 3
        + [pl.BlockSpec(memory_space=pltpu.HBM)] * 3,
        out_specs=pl.BlockSpec(memory_space=pltpu.HBM),
        out_shape=jax.ShapeDtypeStruct(shape, F32),
        scratch_shapes=[
            pltpu.VMEM(shape, F32),
            pltpu.SemaphoreType.DMA((3, 2)),
            pltpu.SemaphoreType.DMA((3, 2)),
        ],
        compiler_params=params(63),
        cost_estimate=COST,
        name="take_moved",
    )(*scalars, *olds)


def keep_kernel(pos, old_starts, new_starts, *refs):
    sources, gradient, out, arrivals = refs[:3], refs[3], refs[4], refs[5]
    copies = []
    for lane in range(2):
        slot = kept_slot(lane, pos[0], old_starts, new_starts)
        there = pl.ds(pl.multiple_of(slot * BLOCK_ROWS, BLOCK_ROWS), BLOCK_ROWS)
        here = pl.ds(lane * BLOCK_ROWS, BLOCK_ROWS)
        copies += [
            pltpu.make_async_copy(source.at[there, :], out.at[i, here, :], arrivals.at[lane, i])
            for i, source in enumerate(sources)
        ]
    for copy in copies:
        copy.start()
    out[3] = gradient[...].astype(F32)
    for copy in copies:
        copy.wait()


def keep_own(scalars, olds, gradient):
    return pl.pallas_call(
        keep_kernel,
        in_specs=[pl.BlockSpec(memory_space=pltpu.SMEM)] * 3
        + [pl.BlockSpec(memory_space=pltpu.HBM)] * 3
        + [pl.BlockSpec(memory_space=pltpu.VMEM)],
        out_shape=jax.ShapeDtypeStruct((4, *gradient.shape), F32),
        scratch_shapes=[pltpu.SemaphoreType.DMA((2, 3))],
        compiler_params=params(),
        cost_estimate=COST,
        name="keep_own",
    )(*scalars, *olds, gradient)


def turn_kernel(seats, pos, block, mine, theirs, turned):
    turned[...] = block[...].T
    core = lax.rem(pos[0], 2)
    for x in range(seats):
        seat = 2 * x
        here = pl.multiple_of((seat + core) * SEAT, SEAT)
        there = pl.multiple_of((seat + 1 - core) * SEAT, SEAT)
        mine[0, x, 0] = turned[pl.ds(here, SEAT), :]
        theirs[0, x, 0] = turned[pl.ds(there, SEAT), :].astype(F32)


def turn_hidden(pos, hidden, groups, seats):
    depth = hidden.shape[0]
    span = 2 * seats * SEAT
    hops = groups // 3
    shape = (3, seats, hops, SEAT, depth)

    def place(z, pos):
        far = lax.rem(z - pos[0] // (2 * seats) + groups, groups)
        return lax.rem(far, 3), 0, z // 3, 0, 0

    block = pl.BlockSpec((1, seats, 1, SEAT, depth), place)
    return pl.pallas_call(
        functools.partial(turn_kernel, seats),
        grid_spec=pltpu.PrefetchScalarGridSpec(
            num_scalar_prefetch=1,
            grid=(groups,),
            in_specs=[pl.BlockSpec((depth, span), lambda z, *_: (0, z))],
            out_specs=[block, block],
            scratch_shapes=[pltpu.VMEM((span, depth), BF16)],
        ),
        out_shape=[jax.ShapeDtypeStruct(shape, BF16), jax.ShapeDtypeStruct(shape, F32)],
        compiler_params=params(),
        cost_estimate=COST,
        name="turn_hidden",
    )(pos, hidden)


def adam_kernel(pos, old_starts, new_starts, kept, moved, *refs):
    new_weight, new_first, new_second, sent = refs
    lane = pl.program_id(0)
    here = pos[0]
    block = new_starts[here] + lane
    arrived = block < jnp.minimum(old_starts[here], new_starts[here + 1])
    live = block < new_starts[here + 1]
    weight_old = jnp.where(arrived, moved[0], kept[0])
    first_old = jnp.where(arrived, moved[1], kept[1])
    second_old = jnp.where(arrived, moved[2], kept[2])
    grad = kept[3]
    first_new = decay_first * first_old + (1.0 - decay_first) * grad
    second_new = decay_second * second_old + (1.0 - decay_second) * grad * grad
    step_dir = (first_new / corr_first) / (jnp.sqrt(second_new / corr_second) + adam_eps)
    weight_next = weight_old - learn_rate * (step_dir + weight_decay * weight_old)
    weight_next = jnp.where(live, weight_next, 0.0)
    new_weight[...] = weight_next
    sent[...] = weight_next
    new_first[...] = jnp.where(live, first_new, 0.0)
    new_second[...] = jnp.where(live, second_new, 0.0)


def adam_step(scalars, kept, moved):
    _, rows, columns = kept.shape

    def arrival(lane, pos, old_starts, new_starts):
        return 0, arrival_slot(lane, pos[0], old_starts, new_starts), 0

    block = (BLOCK_ROWS, columns)
    return pl.pallas_call(
        adam_kernel,
        grid_spec=pltpu.PrefetchScalarGridSpec(
            num_scalar_prefetch=3,
            grid=(2,),
            in_specs=[
                pl.BlockSpec((4, *block), lambda lane, *_: (0, lane, 0)),
                pl.BlockSpec((3, *block), arrival),
            ],
            out_specs=[pl.BlockSpec(block, lambda lane, *_: (lane, 0))] * 4,
        ),
        out_shape=[jax.ShapeDtypeStruct((rows, columns), F32)] * 4,
        compiler_params=params(),
        cost_estimate=COST,
        name="adam_step",
    )(*scalars, kept, moved)


def product_kernel(mine, theirs, weight_mine, weight_theirs, half_a, *half_b):
    sides, seats, rows, _ = mine.shape
    width = half_a.shape[2]
    here = weight_mine[...].astype(BF16)
    there = weight_theirs[...].astype(BF16)
    for side in range(sides):
        for x in range(seats):
            value = jnp.dot(mine[side, x], here, preferred_element_type=F32) + jnp.dot(
                theirs[side, x].astype(BF16), there, preferred_element_type=F32
            )
            half_a[x, side * rows : (side + 1) * rows, :] = value[:, :width]
            half_b[side][x] = value[:, width:]


def products(mine, theirs, weight_mine, weight_theirs):
    sides, seats, rows, _ = mine.shape
    width = weight_mine.shape[1] // 2
    return pl.pallas_call(
        product_kernel,
        out_shape=[jax.ShapeDtypeStruct((seats, sides * rows, width), F32)]
        + [jax.ShapeDtypeStruct((seats, rows, width), F32)] * sides,
        compiler_params=params(),
        cost_estimate=COST,
        name="products",
    )(mine, theirs, weight_mine, weight_theirs)


def add_kernel(*refs):
    value = refs[0][...]
    for ref in refs[1:-1]:
        value = value + ref[...]
    refs[-1][...] = value


def add_up(arrays):
    return pl.pallas_call(
        add_kernel,
        out_shape=jax.ShapeDtypeStruct(arrays[0].shape, F32),
        compiler_params=params(),
        cost_estimate=COST,
        name="add_up",
    )(*arrays)


def split_kernel(stack, *outs):
    rows = outs[0].shape[0]
    for i, out in enumerate(outs):
        out[...] = jnp.sum(stack[:, i * rows : (i + 1) * rows, :], axis=0)


def add_and_split(stack, count):
    _, rows, width = stack.shape
    return pl.pallas_call(
        split_kernel,
        out_shape=[jax.ShapeDtypeStruct((rows // count, width), F32)] * count,
        compiler_params=params(),
        cost_estimate=COST,
        name="add_and_split",
    )(stack)


def merge_kernel(stack, *refs):
    arrays, out = refs[:-1], refs[-1]
    width = stack.shape[2]
    for hop in range(out.shape[0]):
        rows = slice(hop * SEAT, (hop + 1) * SEAT)
        out[hop, :, width:] = jnp.sum(stack[:, rows, :], axis=0)
        value = arrays[0][rows, :]
        for array in arrays[1:]:
            value = value + array[rows, :]
        out[hop, :, :width] = value


def add_and_merge(stack, arrays):
    _, rows, width = stack.shape
    return pl.pallas_call(
        merge_kernel,
        out_shape=jax.ShapeDtypeStruct((rows // SEAT, SEAT, 2 * width), F32),
        compiler_params=params(),
        cost_estimate=COST,
        name="add_and_merge",
    )(stack, *arrays)


def total_kernel(residual, parts, summed, squares):
    square = jnp.zeros((SEAT, 128), F32)
    for start in range(0, residual.shape[1], 128):
        columns = slice(start, start + 128)
        value = residual[:, columns].astype(F32) + jnp.sum(parts[:, :, columns], axis=0)
        summed[:, columns] = value
        square = square + value * value
    row = jnp.sum(square.T, axis=0, keepdims=True)
    row = jnp.concatenate([row] * (128 // SEAT), axis=1)
    squares[...] = jnp.broadcast_to(row[None], squares.shape)


def total_up(residual, parts, peers):
    rows, columns = residual.shape
    return pl.pallas_call(
        total_kernel,
        out_shape=[
            jax.ShapeDtypeStruct((rows, columns), F32),
            jax.ShapeDtypeStruct((peers, 8, 128), F32),
        ],
        compiler_params=params(),
        cost_estimate=COST,
        name="total_up",
    )(residual, parts)


def finish_kernel(features, summed, squares, gain, out):
    row = jnp.sum(squares[...], axis=0)
    scale = lax.rsqrt(row / features + norm_eps)
    wide = jnp.concatenate([scale] * 16, axis=0).T[:SEAT]
    for start in range(0, summed.shape[1], 128):
        columns = slice(start, start + 128)
        out[:, columns] = (summed[:, columns] * wide * gain[:, columns]).astype(BF16)


def finish(summed, squares, gain, features):
    return pl.pallas_call(
        functools.partial(finish_kernel, features),
        out_shape=jax.ShapeDtypeStruct(summed.shape, BF16),
        compiler_params=params(),
        cost_estimate=COST,
        name="finish",
    )(summed, squares, gain.reshape(1, -1))


def on_device(
    old_weight,
    old_first_moment,
    old_second_moment,
    gradient,
    hidden,
    residual,
    norm_gain,
    old_starts,
    new_starts,
):
    columns = old_weight.shape[1]
    width = columns // 2
    groups = lax.axis_size("dp")
    lanes = lax.axis_size("pipe")
    peers = lax.axis_size("tensor")
    seats = lanes // 2
    depth = hidden.shape[0]
    features = columns * peers
    pos = jnp.full((1,), lax.axis_index(DATA), jnp.int32)
    scalars = (pos, old_starts, new_starts)
    olds = (old_weight, old_first_moment, old_second_moment)

    hops = groups // 3
    onward = [(p, p + 1) for p in range(lanes) if p % 4 != 3]
    across = [(p, p ^ 1) for p in range(lanes)]

    by_x = [[2 * x + core for x in range(seats)] for core in range(2)]
    by_hop = [[3 * hop + side for hop in range(hops)] for side in range(3)]

    def spread(array, axis, members):
        return lax.all_to_all(array, axis, 0, 0, axis_index_groups=members)

    def along_z(array, distance):
        route = [(z, (z + distance) % groups) for z in range(groups)]
        return lax.ppermute(array, "dp", route)

    moved = take_moved(scalars, olds)
    after, moved = lax.optimization_barrier((pos, moved))
    moved = lax.ppermute(moved, "pipe", onward)
    mine, theirs = turn_hidden(after, hidden, groups, seats)
    theirs = lax.ppermute(theirs, "pipe", across)
    mine = mine.reshape(3, seats, hops * SEAT, depth)
    theirs = theirs.reshape(3, seats, hops * SEAT, depth)
    kept = keep_own((after, old_starts, new_starts), olds, gradient)

    *state, sent = adam_step(scalars, kept, moved)
    received = lax.ppermute(sent, "pipe", across)
    half_a, first_b, plus_b, minus_b = products(mine, theirs, sent, received)
    half_a = spread(half_a, "pipe", by_x)
    plus_b, minus_b = along_z(plus_b, 1), along_z(minus_b, -1)
    half_a, first_b = lax.optimization_barrier((half_a, first_b))
    half_a = add_and_split(half_a, 3)
    half_a = [half_a[0], along_z(half_a[1], 1), along_z(half_a[2], -1)]
    half_b = spread(add_up([first_b, plus_b, minus_b]), "pipe", by_x)
    parts = spread(add_and_merge(half_b, half_a), "dp", by_hop)
    summed, squares = total_up(residual, parts, peers)
    squares = lax.all_to_all(squares, "tensor", 0, 0)
    layer_out = finish(summed, squares, norm_gain, features)
    return (*state, layer_out)


def solution(mesh):
    data = P(DATA, "tensor")
    return jax.shard_map(
        on_device,
        mesh=mesh,
        in_specs=(data, data, data, data, P(DATA, None), data, P("tensor"), P(), P()),
        out_specs=(data, data, data, data),
        check_vma=False,
    )
```

time: 305 us -> 120 us (0.39)
  waiting for transfers between devices: 234 us -> 27.5 us
  starting transfers between devices: 1.95 us -> 39.9 us
  between operations: 18.8 us -> 0.83 us
  local copies, waits for them, and re-layouts: 20.5 us -> 3.17 us
  blocking collectives: 17 us -> 34.3 us
  Pallas kernels: 0 us -> 13.4 us
  other arithmetic: 8.25 us -> 0 us
  matrix products: 3.64 us -> 0 us
    unnamed x2 -> x0, waiting for transfers between devices: 223 us -> none
    all_to_all x0 -> x2, blocking collectives: none -> 34.3 us  [the longest x1 19.4 us: spread(): return lax.all_to_all(array, axis, 0, 0, axis_index_groups=members)]
    ppermute x1 -> x7, starting transfers between devices: 1.91 us -> 30.6 us  [the longest x4 24.7 us: along_z(): return lax.ppermute(array, 'dp', route)]
    psum x1 -> x0, blocking collectives: 17 us -> none  [on_device(): row_total = lax.psum(jnp.sum(summed * summed, axis=1), 'tensor')]
    ppermute x1 -> x7, waiting for transfers between devices: 11.1 us -> 24.8 us  [the longest x1 11.9 us: on_device(): moved = lax.ppermute(moved, 'pipe', onward)]
    pallas_call x0 -> x10, Pallas kernels: none -> 13.4 us  [the longest x1 3.29 us: take_moved(): pl.pallas_call(take_kernel, in_specs=[pl.BlockSpec(memory_space=pltpu.SME...]
    all_to_all x0 -> x2, starting transfers between devices: none -> 9.3 us  [spread(): return lax.all_to_all(array, axis, 0, 0, axis_index_groups=members)]
    gather x6 -> x0, local copies, waits for them, and re-layouts: 9.16 us -> none  [select_blocks(): chosen = jnp.take(blocks, slot_ids, axis=0)]
  transfers between devices with their start and end apart: 2 -> 9, of which waited for: 2 -> 7; matrix products, arithmetic and copies ran while one was open for 2% -> 0% of each run, Pallas kernels for 0% -> 5%
where the time goes in v1:
time: 120 us; the launch traced here: 119 us
  starting transfers between devices  39.9 us (33%)
  blocking collectives  34.3 us (29%)
  waiting for transfers between devices  27.5 us (23%)
  Pallas kernels  13.4 us (11%)
  local copies, waits for them, and re-layouts  3.17 us (3%)
    ppermute x4, starting transfers between devices, along_z(): return lax.ppermute(array, 'dp', route)  24.7 us
    all_to_all x1, blocking collectives, spread(): return lax.all_to_all(array, axis, 0, 0, axis_index_groups=members)  19.4 us
    all_to_all x1, blocking collectives, on_device(): squares = lax.all_to_all(squares, 'tensor', 0, 0)  14.9 us
    ppermute x1, waiting for transfers between devices, on_device(): moved = lax.ppermute(moved, 'pipe', onward)  11.9 us
    ppermute x4, waiting for transfers between devices, along_z(): return lax.ppermute(array, 'dp', route)  11 us
    all_to_all x2, starting transfers between devices, spread(): return lax.all_to_all(array, axis, 0, 0, axis_index_groups=members)  9.3 us
    pallas_call x1, Pallas kernels, take_moved(): pl.pallas_call(take_kernel, in_specs=[pl.BlockSpec(memory_space=pltpu.SME...  3.29 us
    unnamed x20, local copies, waits for them, and re-layouts  3.17 us
  transfers between devices with their start and end apart: 9, of which 7 were waited for; matrix products, arithmetic and copies ran while one was open for 0% of the time, Pallas kernels for 5%

profile of v1, /device:TPU:6, one launch (start us, length us, event | category | flops | bytes accessed | tf_op | source)
XLA Modules:
  0.0 119.1 jit_solution(3679452679759044717)
XLA Ops:
  0.6 0.0 copy-start.2
  0.7 3.3 %take_moved.1 = f32[3,256,512]{2,1,0:T(8,128)} custom-call(s32[1]{0:T(128)} %bitcast.pos, s32[97]{0:T(128)} %old_starts.5, s32[97]{0:T(128)} %new_starts.5, f32[384,512]{1,0:T(8,128)} %refs_0_.3, f32[384,512]{1,0:T(8,128)} %refs_1_.3, f32[384,512]{1,0:T(8,128)} %refs_2_.3), custom_call_target="tpu_custom_call" | custom-call | bytes 1024 | tf_op jit(solution)/shard_map/take_moved/pallas_call | solution.py:83
  4.0 0.0 copy-start
  4.0 0.0 copy-start.1
  4.0 2.1 %collective-permute-start = (f32[3,256,512]{2,1,0:T(8,128)}, f32[3,256,512]{2,1,0:T(8,128)S(1)}, u32[]{:S(2)}, u32[]{:S(2)}) collective-permute-start(f32[3,256,512]{2,1,0:T(8,128)} %take_moved.1), channel_id=1, source_target_pairs={{0,1},{1,2},{2,3},{4,5},{5,6},{6,7},{8,9},{9,10},{10,11},{12,13},{... | collective-permute-start | bytes 4718600 | tf_op jit(solution)/shard_map/ppermute | solution.py:385
  6.0 0.0 copy-start.3
  6.0 1.4 %copy-done.3 = bf16[256,3072]{1,0:T(8,128)(2,1)S(1)} copy-done((bf16[256,3072]{1,0:T(8,128)(2,1)S(1)}, bf16[256,3072]{1,0:T(8,128)(2,1)}, u32[]{:S(2)}) %copy-start.3) | copy-done | bytes 1572888
  7.4 0.0 copy-start.6
  7.4 0.0 copy-start.7
  7.4 3.0 %turn_hidden.1 = (bf16[3,4,4,32,256]{4,3,2,1,0:T(8,128)(2,1)S(1)}, f32[3,4,4,32,256]{4,3,2,1,0:T(8,128)S(1)}) custom-call(s32[1]{0:T(128)} %bitcast.pos, bf16[256,3072]{1,0:T(8,128)(2,1)S(1)} %copy-done.3), custom_call_target="tpu_custom_call" | custom-call | bytes 1024 | tf_op jit(solution)/shard_map/turn_hidden/pallas_call | solution.py:154
  10.5 1.9 %collective-permute-start.1 = (f32[3,4,4,32,256]{4,3,2,1,0:T(8,128)S(1)}, f32[3,4,4,32,256]{4,3,2,1,0:T(8,128)S(1)}, u32[]{:S(2)}, u32[]{:S(2)}) collective-permute-start(f32[3,4,4,32,256]{4,3,2,1,0:T(8,128)S(1)} %get-tuple-element.29), channel_id=1, source_target_pairs={{0,1},{1,0},{2,3},{3,2},{4,5},{5,4},{6,7},{7,6},{8,9},{9,8},{10,11... | collective-permute-start | bytes 4718600 | tf_op jit(solution)/shard_map/ppermute | solution.py:387
  12.4 0.0 copy-done.2
  12.4 0.0 copy-done
  12.4 0.0 copy-done.1
  12.4 0.0 copy-done.6
  12.4 0.0 copy-done.7
  12.5 0.0 copy-start.4
  12.5 0.9 copy-done.4
  13.4 0.8 keep_own.1.kept
  14.2 11.9 %collective-permute-done.moved = f32[3,256,512]{2,1,0:T(8,128)S(1)} collective-permute-done((f32[3,256,512]{2,1,0:T(8,128)}, f32[3,256,512]{2,1,0:T(8,128)S(1)}, u32[]{:S(2)}, u32[]{:S(2)}) %collective-permute-start) | collective-permute-done | bytes 1572896 | tf_op jit(solution)/shard_map/ppermute | solution.py:385
  26.1 2.3 %adam_step.1 = (f32[256,512]{1,0:T(8,128)}, f32[256,512]{1,0:T(8,128)}, f32[256,512]{1,0:T(8,128)}, f32[256,512]{1,0:T(8,128)S(1)}) custom-call(s32[1]{0:T(128)} %bitcast.pos, s32[97]{0:T(128)S(1)} %copy-done.6, s32[97]{0:T(128)S(1)} %copy-done.7, f32[4,256,512]{2,1,0:T(8,128)S(1)} %keep_own.1.kept, f32[3,256,512]{2,1,0:T(8,128)S(1)} %collective-permute-done.moved), custom_call_target="tpu_custom_call" | custom-call | bytes 1024 | tf_op jit(solution)/shard_map/adam_step/pallas_call | solution.py:199
  28.3 1.9 %collective-permute-start.2 = (f32[256,512]{1,0:T(8,128)S(1)}, f32[256,512]{1,0:T(8,128)S(1)}, u32[]{:S(2)}, u32[]{:S(2)}) collective-permute-start(f32[256,512]{1,0:T(8,128)S(1)} %get-tuple-element.30.weight_mine), channel_id=1, source_target_pairs={{0,1},{1,0},{2,3},{3,2},{4,5},{5,4},{6,7},{7,6},{8,9},{9,8},{10,11... | collective-permute-start | bytes 1572872 | tf_op jit(solution)/shard_map/ppermute | solution.py:393
  30.3 0.0 collective-permute-done.1
  30.3 1.9 %collective-permute-done.2.weight_theirs = f32[256,512]{1,0:T(8,128)S(1)} collective-permute-done((f32[256,512]{1,0:T(8,128)S(1)}, f32[256,512]{1,0:T(8,128)S(1)}, u32[]{:S(2)}, u32[]{:S(2)}) %collective-permute-start.2) | collective-permute-done | bytes 524320 | tf_op jit(solution)/shard_map/ppermute | solution.py:393
  32.1 2.2 %products.1 = (f32[4,384,256]{2,1,0:T(8,128)}, f32[4,128,256]{2,1,0:T(8,128)S(1)}, f32[4,128,256]{2,1,0:T(8,128)}, f32[4,128,256]{2,1,0:T(8,128)S(1)}) custom-call(bf16[3,4,128,256]{3,2,1,0:T(8,128)(2,1)S(1)} %bitcast.5, f32[3,4,128,256]{3,2,1,0:T(8,128)S(1)} %bitcast.4, f32[256,512]{1,0:T(8,128)S(1)} %get-tuple-element.30.weight_mine, ...), custom_call_target="tpu_custom_call" | custom-call | bytes 1024 | tf_op jit(solution)/shard_map/products/pallas_call | solution.py:234
  34.3 0.0 copy-start.9
  34.3 0.8 copy-done.9
  35.1 4.5 %all-to-all-start = ((f32[4,384,256]{2,1,0:T(8,128)}), f32[4,384,256]{2,1,0:T(8,128)S(1)}, u32[]{:S(2)}, u32[]{:S(2)}) async-start(f32[4,384,256]{2,1,0:T(8,128)} %get-tuple-element.31), calls=%async_computation | async-start | bytes 3145728 | tf_op jit(solution)/shard_map/all_to_all | solution.py:377
  39.6 4.0 %collective-permute-start.3 = (f32[4,128,256]{2,1,0:T(8,128)}, f32[4,128,256]{2,1,0:T(8,128)S(1)}, u32[]{:S(2)}, u32[]{:S(2)}) collective-permute-start(f32[4,128,256]{2,1,0:T(8,128)} %get-tuple-element.34), channel_id=1, source_target_pairs={{0,64},{64,128},{128,192},{192,256},{256,320},{320,384},{384,448},... | collective-permute-start | bytes 1572872 | tf_op jit(solution)/shard_map/ppermute | solution.py:381
  43.6 12.2 %collective-permute-start.4 = (f32[4,128,256]{2,1,0:T(8,128)}, f32[4,128,256]{2,1,0:T(8,128)S(1)}, u32[]{:S(2)}, u32[]{:S(2)}) collective-permute-start(f32[4,128,256]{2,1,0:T(8,128)} %copy-done.9), channel_id=1, source_target_pairs={{0,704},{64,0},{128,64},{192,128},{256,192},{320,256},{384,320},{4... | collective-permute-start | bytes 1572872 | tf_op jit(solution)/shard_map/ppermute | solution.py:381
  55.9 2.7 %all-to-all-done.stack = f32[4,384,256]{2,1,0:T(8,128)S(1)} async-done(((f32[4,384,256]{2,1,0:T(8,128)}), f32[4,384,256]{2,1,0:T(8,128)S(1)}, u32[]{:S(2)}, u32[]{:S(2)}) %all-to-all-start) | async-done | bytes 1572896 | tf_op jit(solution)/shard_map/all_to_all | solution.py:377
  58.5 7.2 %collective-permute-done.3.refs_1_ = f32[4,128,256]{2,1,0:T(8,128)S(1)} collective-permute-done((f32[4,128,256]{2,1,0:T(8,128)}, f32[4,128,256]{2,1,0:T(8,128)S(1)}, u32[]{:S(2)}, u32[]{:S(2)}) %collective-permute-start.3) | collective-permute-done | bytes 524320 | tf_op jit(solution)/shard_map/ppermute | solution.py:381
  65.8 1.3 %collective-permute-done.4.refs_2_ = f32[4,128,256]{2,1,0:T(8,128)S(1)} collective-permute-done((f32[4,128,256]{2,1,0:T(8,128)}, f32[4,128,256]{2,1,0:T(8,128)S(1)}, u32[]{:S(2)}, u32[]{:S(2)}) %collective-permute-start.4) | collective-permute-done | bytes 524320 | tf_op jit(solution)/shard_map/ppermute | solution.py:381
  67.1 0.9 add_up.1
  68.0 4.8 %all-to-all-start.1 = ((f32[4,128,256]{2,1,0:T(8,128)}), f32[4,128,256]{2,1,0:T(8,128)S(1)}, u32[]{:S(2)}, u32[]{:S(2)}) async-start(f32[4,128,256]{2,1,0:T(8,128)} %add_up.1), calls=%async_computation.1 | async-start | bytes 1048576 | tf_op jit(solution)/shard_map/all_to_all | solution.py:377
  72.8 0.0 copy-start.5
  72.8 0.0 copy-start.8
  72.8 0.1 add_and_split.1
  72.8 1.9 %collective-permute-start.5 = (f32[128,256]{1,0:T(8,128)S(1)}, f32[128,256]{1,0:T(8,128)S(1)}, u32[]{:S(2)}, u32[]{:S(2)}) collective-permute-start(f32[128,256]{1,0:T(8,128)S(1)} %get-tuple-element.38), channel_id=1, source_target_pairs={{0,64},{64,128},{128,192},{192,256},{256,320},{320,384},{384,448},... | collective-permute-start | bytes 393224 | tf_op jit(solution)/shard_map/ppermute | solution.py:381
  74.8 6.5 %collective-permute-start.6 = (f32[128,256]{1,0:T(8,128)S(1)}, f32[128,256]{1,0:T(8,128)S(1)}, u32[]{:S(2)}, u32[]{:S(2)}) collective-permute-start(f32[128,256]{1,0:T(8,128)S(1)} %get-tuple-element.39), channel_id=1, source_target_pairs={{0,704},{64,0},{128,64},{192,128},{256,192},{320,256},{384,320},{4... | collective-permute-start | bytes 393224 | tf_op jit(solution)/shard_map/ppermute | solution.py:381
  81.3 1.0 collective-permute-done.5.refs_1_
  82.3 1.5 %collective-permute-done.6.refs_2_ = f32[128,256]{1,0:T(8,128)S(1)} collective-permute-done((f32[128,256]{1,0:T(8,128)S(1)}, f32[128,256]{1,0:T(8,128)S(1)}, u32[]{:S(2)}, u32[]{:S(2)}) %collective-permute-start.6) | collective-permute-done | bytes 131104 | tf_op jit(solution)/shard_map/ppermute | solution.py:381
  83.8 0.0 all-to-all-done.1.stack
  83.8 19.4 %all_to_all.20.parts = f32[4,32,512]{2,1,0:T(8,128)S(1)} all-to-all(f32[4,32,512]{2,1,0:T(8,128)S(1)} %add_and_merge.1), channel_id=1, replica_groups={{0,192,384,576},{64,256,448,640},{128,320,512,704},{1,193,385,577},{65,..., dimensions={0} | all-to-all | bytes 524288 | tf_op jit(solution)/shard_map/all_to_all | solution.py:377
  103.2 0.0 copy-done.5
  103.2 0.2 total_up.1
  103.4 14.9 %all_to_all.21.squares = f32[8,8,128]{2,1,0:T(8,128)S(1)} all-to-all(f32[8,8,128]{2,1,0:T(8,128)S(1)} %get-tuple-element.41), channel_id=1, replica_groups=mesh['dp'=12,'tensor'=8,'pipe'=8] {'tensor'}, dimensions={0} | all-to-all | bytes 65536 | tf_op jit(solution)/shard_map/all_to_all | solution.py:403
  118.4 0.0 copy-done.8
  118.4 0.7 finish.1
  (1 shorter events, 0.0 us)
Async XLA Ops:
  0.6 11.8 %copy-start.2 = (f32[384,512]{1,0:T(8,128)S(1)}, f32[384,512]{1,0:T(8,128)}, u32[]{:S(2)}) copy-start(f32[384,512]{1,0:T(8,128)} %refs_2_.3) | copy-start | bytes 2359300
  4.0 8.5 %copy-start = (f32[384,512]{1,0:T(8,128)S(1)}, f32[384,512]{1,0:T(8,128)}, u32[]{:S(2)}) copy-start(f32[384,512]{1,0:T(8,128)} %refs_0_.3) | copy-start | bytes 2359300
  4.0 8.5 %copy-start.1 = (f32[384,512]{1,0:T(8,128)S(1)}, f32[384,512]{1,0:T(8,128)}, u32[]{:S(2)}) copy-start(f32[384,512]{1,0:T(8,128)} %refs_1_.3) | copy-start | bytes 2359300
  4.0 22.1 %collective-permute-start = (f32[3,256,512]{2,1,0:T(8,128)}, f32[3,256,512]{2,1,0:T(8,128)S(1)}, u32[]{:S(2)}, u32[]{:S(2)}) collective-permute-start(f32[3,256,512]{2,1,0:T(8,128)} %take_moved.1), channel_id=1, source_target_pairs={{0,1},{1,2},{2,3},{4,5},{5,6},{6,7},{8,9},{9,10},{10,11},{12,13},{... | collective-permute-start | bytes 4718600 | tf_op jit(solution)/shard_map/ppermute | solution.py:385
  6.0 1.4 %copy-start.3 = (bf16[256,3072]{1,0:T(8,128)(2,1)S(1)}, bf16[256,3072]{1,0:T(8,128)(2,1)}, u32[]{:S(2)}) copy-start(bf16[256,3072]{1,0:T(8,128)(2,1)} %block.1) | copy-start | bytes 4718596
  7.4 5.0 %copy-start.6 = (s32[97]{0:T(128)S(1)}, s32[97]{0:T(128)}, u32[]{:S(2)}) copy-start(s32[97]{0:T(128)} %old_starts.5) | copy-start | bytes 1168
  7.4 5.0 %copy-start.7 = (s32[97]{0:T(128)S(1)}, s32[97]{0:T(128)}, u32[]{:S(2)}) copy-start(s32[97]{0:T(128)} %new_starts.5) | copy-start | bytes 1168
  10.5 19.8 %collective-permute-start.1 = (f32[3,4,4,32,256]{4,3,2,1,0:T(8,128)S(1)}, f32[3,4,4,32,256]{4,3,2,1,0:T(8,128)S(1)}, u32[]{:S(2)}, u32[]{:S(2)}) collective-permute-start(f32[3,4,4,32,256]{4,3,2,1,0:T(8,128)S(1)} %get-tuple-element.29), channel_id=1, source_target_pairs={{0,1},{1,0},{2,3},{3,2},{4,5},{5,4},{6,7},{7,6},{8,9},{9,8},{10,11... | collective-permute-start | bytes 4718600 | tf_op jit(solution)/shard_map/ppermute | solution.py:387
  12.5 1.0 copy-start.4
  28.3 3.8 %collective-permute-start.2 = (f32[256,512]{1,0:T(8,128)S(1)}, f32[256,512]{1,0:T(8,128)S(1)}, u32[]{:S(2)}, u32[]{:S(2)}) collective-permute-start(f32[256,512]{1,0:T(8,128)S(1)} %get-tuple-element.30.weight_mine), channel_id=1, source_target_pairs={{0,1},{1,0},{2,3},{3,2},{4,5},{5,4},{6,7},{7,6},{8,9},{9,8},{10,11... | collective-permute-start | bytes 1572872 | tf_op jit(solution)/shard_map/ppermute | solution.py:393
  34.3 0.8 copy-start.9
  35.1 23.5 %all-to-all-start = ((f32[4,384,256]{2,1,0:T(8,128)}), f32[4,384,256]{2,1,0:T(8,128)S(1)}, u32[]{:S(2)}, u32[]{:S(2)}) async-start(f32[4,384,256]{2,1,0:T(8,128)} %get-tuple-element.31), calls=%async_computation | async-start | bytes 3145728 | tf_op jit(solution)/shard_map/all_to_all | solution.py:377
  39.6 26.2 %collective-permute-start.3 = (f32[4,128,256]{2,1,0:T(8,128)}, f32[4,128,256]{2,1,0:T(8,128)S(1)}, u32[]{:S(2)}, u32[]{:S(2)}) collective-permute-start(f32[4,128,256]{2,1,0:T(8,128)} %get-tuple-element.34), channel_id=1, source_target_pairs={{0,64},{64,128},{128,192},{192,256},{256,320},{320,384},{384,448},... | collective-permute-start | bytes 1572872 | tf_op jit(solution)/shard_map/ppermute | solution.py:381
  43.6 23.4 %collective-permute-start.4 = (f32[4,128,256]{2,1,0:T(8,128)}, f32[4,128,256]{2,1,0:T(8,128)S(1)}, u32[]{:S(2)}, u32[]{:S(2)}) collective-permute-start(f32[4,128,256]{2,1,0:T(8,128)} %copy-done.9), channel_id=1, source_target_pairs={{0,704},{64,0},{128,64},{192,128},{256,192},{320,256},{384,320},{4... | collective-permute-start | bytes 1572872 | tf_op jit(solution)/shard_map/ppermute | solution.py:381
  68.0 15.8 %all-to-all-start.1 = ((f32[4,128,256]{2,1,0:T(8,128)}), f32[4,128,256]{2,1,0:T(8,128)S(1)}, u32[]{:S(2)}, u32[]{:S(2)}) async-start(f32[4,128,256]{2,1,0:T(8,128)} %add_up.1), calls=%async_computation.1 | async-start | bytes 1048576 | tf_op jit(solution)/shard_map/all_to_all | solution.py:377
  72.8 30.5 %copy-start.5 = (bf16[32,512]{1,0:T(8,128)(2,1)S(1)}, bf16[32,512]{1,0:T(8,128)(2,1)}, u32[]{:S(2)}) copy-start(bf16[32,512]{1,0:T(8,128)(2,1)} %residual.1) | copy-start | bytes 98308
  72.8 45.6 %copy-start.8 = (f32[512]{0:T(512)S(1)}, f32[512]{0:T(512)}, u32[]{:S(2)}) copy-start(f32[512]{0:T(512)} %param.15) | copy-start | bytes 6148
  72.8 9.5 %collective-permute-start.5 = (f32[128,256]{1,0:T(8,128)S(1)}, f32[128,256]{1,0:T(8,128)S(1)}, u32[]{:S(2)}, u32[]{:S(2)}) collective-permute-start(f32[128,256]{1,0:T(8,128)S(1)} %get-tuple-element.38), channel_id=1, source_target_pairs={{0,64},{64,128},{128,192},{192,256},{256,320},{320,384},{384,448},... | collective-permute-start | bytes 393224 | tf_op jit(solution)/shard_map/ppermute | solution.py:381
  74.8 9.0 %collective-permute-start.6 = (f32[128,256]{1,0:T(8,128)S(1)}, f32[128,256]{1,0:T(8,128)S(1)}, u32[]{:S(2)}, u32[]{:S(2)}) collective-permute-start(f32[128,256]{1,0:T(8,128)S(1)} %get-tuple-element.39), channel_id=1, source_target_pairs={{0,704},{64,0},{128,64},{192,128},{256,192},{320,256},{384,320},{4... | collective-permute-start | bytes 393224 | tf_op jit(solution)/shard_map/ppermute | solution.py:381

commit v2 on v1

--- a/solution.py
+++ b/solution.py
@@ -131,13 +131,15 @@
 
 def turn_kernel(seats, pos, block, mine, theirs, turned):
     turned[...] = block[...].T
+    here_x = lax.rem(pos[0], 2 * seats) // 2
     core = lax.rem(pos[0], 2)
-    for x in range(seats):
+    for away in range(seats):
+        x = lax.rem(here_x + away, seats)
         seat = 2 * x
         here = pl.multiple_of((seat + core) * SEAT, SEAT)
         there = pl.multiple_of((seat + 1 - core) * SEAT, SEAT)
-        mine[0, x, 0] = turned[pl.ds(here, SEAT), :]
-        theirs[0, x, 0] = turned[pl.ds(there, SEAT), :].astype(F32)
+        mine[0, away, 0] = turned[pl.ds(here, SEAT), :]
+        theirs[0, away, 0] = turned[pl.ds(there, SEAT), :].astype(F32)
 
 
 def turn_hidden(pos, hidden, groups, seats):
@@ -167,65 +169,55 @@
     )(pos, hidden)
 
 
-def adam_kernel(pos, old_starts, new_starts, kept, moved, *refs):
-    new_weight, new_first, new_second, sent = refs
-    lane = pl.program_id(0)
+def adam_kernel(pos, old_starts, new_starts, kept, moved, new_weight, *moments):
     here = pos[0]
-    block = new_starts[here] + lane
-    arrived = block < jnp.minimum(old_starts[here], new_starts[here + 1])
-    live = block < new_starts[here + 1]
-    weight_old = jnp.where(arrived, moved[0], kept[0])
-    first_old = jnp.where(arrived, moved[1], kept[1])
-    second_old = jnp.where(arrived, moved[2], kept[2])
-    grad = kept[3]
-    first_new = decay_first * first_old + (1.0 - decay_first) * grad
-    second_new = decay_second * second_old + (1.0 - decay_second) * grad * grad
-    step_dir = (first_new / corr_first) / (jnp.sqrt(second_new / corr_second) + adam_eps)
-    weight_next = weight_old - learn_rate * (step_dir + weight_decay * weight_old)
-    weight_next = jnp.where(live, weight_next, 0.0)
-    new_weight[...] = weight_next
-    sent[...] = weight_next
-    new_first[...] = jnp.where(live, first_new, 0.0)
-    new_second[...] = jnp.where(live, second_new, 0.0)
-
-
-def adam_step(scalars, kept, moved):
-    _, rows, columns = kept.shape
-
-    def arrival(lane, pos, old_starts, new_starts):
-        return 0, arrival_slot(lane, pos[0], old_starts, new_starts), 0
-
-    block = (BLOCK_ROWS, columns)
+    for lane in range(2):
+        block = new_starts[here] + lane
+        arrived = block < jnp.minimum(old_starts[here], new_starts[here + 1])
+        live = block < new_starts[here + 1]
+        slot = arrival_slot(lane, here, old_starts, new_starts)
+        there = pl.ds(pl.multiple_of(slot * BLOCK_ROWS, BLOCK_ROWS), BLOCK_ROWS)
+        rows = slice(lane * BLOCK_ROWS, (lane + 1) * BLOCK_ROWS)
+        weight_old = jnp.where(arrived, moved[0, there, :], kept[0, rows, :])
+        first_old = jnp.where(arrived, moved[1, there, :], kept[1, rows, :])
+        second_old = jnp.where(arrived, moved[2, there, :], kept[2, rows, :])
+        grad = kept[3, rows, :]
+        first_new = decay_first * first_old + (1.0 - decay_first) * grad
+        second_new = decay_second * second_old + (1.0 - decay_second) * grad * grad
+        step_dir = (first_new / corr_first) / (jnp.sqrt(second_new / corr_second) + adam_eps)
+        weight_next = weight_old - learn_rate * (step_dir + weight_decay * weight_old)
+        new_weight[rows, :] = jnp.where(live, weight_next, 0.0)
+        if moments:
+            new_first, new_second = moments
+            new_first[rows, :] = jnp.where(live, first_new, 0.0)
+            new_second[rows, :] = jnp.where(live, second_new, 0.0)
+
+
+def adam_step(scalars, kept, moved, count):
     return pl.pallas_call(
         adam_kernel,
-        grid_spec=pltpu.PrefetchScalarGridSpec(
-            num_scalar_prefetch=3,
-            grid=(2,),
-            in_specs=[
-                pl.BlockSpec((4, *block), lambda lane, *_: (0, lane, 0)),
-                pl.BlockSpec((3, *block), arrival),
-            ],
-            out_specs=[pl.BlockSpec(block, lambda lane, *_: (lane, 0))] * 4,
-        ),
-        out_shape=[jax.ShapeDtypeStruct((rows, columns), F32)] * 4,
+        in_specs=[pl.BlockSpec(memory_space=pltpu.SMEM)] * 3
+        + [pl.BlockSpec(memory_space=pltpu.VMEM)] * 2,
+        out_shape=[jax.ShapeDtypeStruct(kept.shape[1:], F32)] * count,
         compiler_params=params(),
         cost_estimate=COST,
         name="adam_step",
     )(*scalars, kept, moved)
 
 
-def product_kernel(mine, theirs, weight_mine, weight_theirs, half_a, *half_b):
+def product_kernel(mine, theirs, weight_mine, weight_theirs, *outs):
     sides, seats, rows, _ = mine.shape
-    width = half_a.shape[2]
+    halves_a, halves_b = outs[:seats], outs[seats:]
+    width = halves_a[0].shape[1]
     here = weight_mine[...].astype(BF16)
     there = weight_theirs[...].astype(BF16)
-    for side in range(sides):
-        for x in range(seats):
-            value = jnp.dot(mine[side, x], here, preferred_element_type=F32) + jnp.dot(
-                theirs[side, x].astype(BF16), there, preferred_element_type=F32
+    for away in range(seats):
+        for side in range(sides):
+            value = jnp.dot(mine[side, away], here, preferred_element_type=F32) + jnp.dot(
+                theirs[side, away].astype(BF16), there, preferred_element_type=F32
             )
-            half_a[x, side * rows : (side + 1) * rows, :] = value[:, :width]
-            half_b[side][x] = value[:, width:]
+            halves_a[away][side * rows : (side + 1) * rows, :] = value[:, :width]
+            halves_b[side][away] = value[:, width:]
 
 
 def products(mine, theirs, weight_mine, weight_theirs):
@@ -233,7 +225,7 @@
     width = weight_mine.shape[1] // 2
     return pl.pallas_call(
         product_kernel,
-        out_shape=[jax.ShapeDtypeStruct((seats, sides * rows, width), F32)]
+        out_shape=[jax.ShapeDtypeStruct((sides * rows, width), F32)] * seats
         + [jax.ShapeDtypeStruct((seats, rows, width), F32)] * sides,
         compiler_params=params(),
         cost_estimate=COST,
@@ -241,42 +233,53 @@
     )(mine, theirs, weight_mine, weight_theirs)
 
 
-def add_kernel(*refs):
-    value = refs[0][...]
-    for ref in refs[1:-1]:
-        value = value + ref[...]
-    refs[-1][...] = value
-
-
-def add_up(arrays):
+def add_kernel(pos, *refs):
+    out = refs[-1]
+    seats = out.shape[0]
+    seat = lax.rem(pos[0], 2 * seats) // 2
+    for away in range(seats):
+        value = refs[0][away]
+        for ref in refs[1:-1]:
+            value = value + ref[away]
+        out[lax.rem(seat + away, seats)] = value
+
+
+def add_up(pos, arrays):
     return pl.pallas_call(
         add_kernel,
+        in_specs=[pl.BlockSpec(memory_space=pltpu.SMEM)]
+        + [pl.BlockSpec(memory_space=pltpu.VMEM)] * len(arrays),
         out_shape=jax.ShapeDtypeStruct(arrays[0].shape, F32),
         compiler_params=params(),
         cost_estimate=COST,
         name="add_up",
-    )(*arrays)
-
-
-def split_kernel(stack, *outs):
+    )(pos, *arrays)
+
+
+def split_kernel(count, *refs):
+    outs = refs[count:]
     rows = outs[0].shape[0]
     for i, out in enumerate(outs):
-        out[...] = jnp.sum(stack[:, i * rows : (i + 1) * rows, :], axis=0)
-
-
-def add_and_split(stack, count):
-    _, rows, width = stack.shape
-    return pl.pallas_call(
-        split_kernel,
+        part = slice(i * rows, (i + 1) * rows)
+        value = refs[0][part, :]
+        for ref in refs[1:count]:
+            value = value + ref[part, :]
+        out[...] = value
+
+
+def add_and_split(arrays, count):
+    rows, width = arrays[0].shape
+    return pl.pallas_call(
+        functools.partial(split_kernel, len(arrays)),
         out_shape=[jax.ShapeDtypeStruct((rows // count, width), F32)] * count,
         compiler_params=params(),
         cost_estimate=COST,
         name="add_and_split",
-    )(stack)
-
-
-def merge_kernel(stack, *refs):
-    arrays, out = refs[:-1], refs[-1]
+    )(*arrays)
+
+
+def merge_kernel(*refs):
+    arrays, stack, out = refs[:-2], refs[-2], refs[-1]
     width = stack.shape[2]
     for hop in range(out.shape[0]):
         rows = slice(hop * SEAT, (hop + 1) * SEAT)
@@ -295,7 +298,7 @@
         compiler_params=params(),
         cost_estimate=COST,
         name="add_and_merge",
-    )(stack, *arrays)
+    )(*arrays, stack)
 
 
 def total_kernel(residual, parts, summed, squares):
@@ -316,7 +319,7 @@
         total_kernel,
         out_shape=[
             jax.ShapeDtypeStruct((rows, columns), F32),
-            jax.ShapeDtypeStruct((peers, 8, 128), F32),
+            jax.ShapeDtypeStruct((peers, 1, 128), F32),
         ],
         compiler_params=params(),
         cost_estimate=COST,
@@ -325,7 +328,7 @@
 
 
 def finish_kernel(features, summed, squares, gain, out):
-    row = jnp.sum(squares[...], axis=0)
+    row = jnp.broadcast_to(jnp.sum(squares[...], axis=0), (8, 128))
     scale = lax.rsqrt(row / features + norm_eps)
     wide = jnp.concatenate([scale] * 16, axis=0).T[:SEAT]
     for start in range(0, summed.shape[1], 128):
@@ -370,6 +373,10 @@
     onward = [(p, p + 1) for p in range(lanes) if p % 4 != 3]
     across = [(p, p ^ 1) for p in range(lanes)]
 
+    def along_x(array, distance):
+        route = [(p, (p + 2 * distance) % lanes) for p in range(lanes)]
+        return lax.ppermute(array, "pipe", route)
+
     by_x = [[2 * x + core for x in range(seats)] for core in range(2)]
     by_hop = [[3 * hop + side for hop in range(hops)] for side in range(3)]
 
@@ -389,15 +396,16 @@
     theirs = theirs.reshape(3, seats, hops * SEAT, depth)
     kept = keep_own((after, old_starts, new_starts), olds, gradient)
 
-    *state, sent = adam_step(scalars, kept, moved)
+    (sent,) = adam_step(scalars, kept, moved, 1)
     received = lax.ppermute(sent, "pipe", across)
-    half_a, first_b, plus_b, minus_b = products(mine, theirs, sent, received)
-    half_a = spread(half_a, "pipe", by_x)
+    state = adam_step(scalars, kept, moved, 3)
+    mine, *state = lax.optimization_barrier((mine, *state))
+    *half_a, first_b, plus_b, minus_b = products(mine, theirs, sent, received)
     plus_b, minus_b = along_z(plus_b, 1), along_z(minus_b, -1)
-    half_a, first_b = lax.optimization_barrier((half_a, first_b))
+    half_a = [half_a[0], *(along_x(half_a[away], away) for away in (2, 1, 3))]
+    half_b = spread(add_up(pos, [first_b, plus_b, minus_b]), "pipe", by_x)
     half_a = add_and_split(half_a, 3)
     half_a = [half_a[0], along_z(half_a[1], 1), along_z(half_a[2], -1)]
-    half_b = spread(add_up([first_b, plus_b, minus_b]), "pipe", by_x)
     parts = spread(add_and_merge(half_b, half_a), "dp", by_hop)
     summed, squares = total_up(residual, parts, peers)
     squares = lax.all_to_all(squares, "tensor", 0, 0)

time: 120 us -> 119 us (level)
  waiting for transfers between devices: 27.5 us -> 23.3 us
  starting transfers between devices: 39.9 us -> 42.9 us
  blocking collectives: 34.3 us -> 35.5 us
    ppermute x0 -> x3, starting transfers between devices: none -> 8.91 us  [along_x(): return lax.ppermute(array, 'pipe', route)]
    ppermute x0 -> x3, waiting for transfers between devices: none -> 5.95 us  [along_x(): return lax.ppermute(array, 'pipe', route)]
    ppermute x4, waiting for transfers between devices: 11 us -> 5.44 us  [along_z(): return lax.ppermute(array, 'dp', route)]
    all_to_all x2 -> x1, starting transfers between devices: 9.3 us -> 4.5 us  [spread(): return lax.all_to_all(array, axis, 0, 0, axis_index_groups=members)]
    all_to_all x2 -> x1, waiting for transfers between devices: 2.69 us -> 0.01 us  [spread(): return lax.all_to_all(array, axis, 0, 0, axis_index_groups=members)]
    ppermute x1, waiting for transfers between devices: 1.87 us -> 0.01 us  [on_device(): received = lax.ppermute(sent, 'pipe', across)]
    all_to_all x1, blocking collectives: 19.4 us -> 20.9 us  [spread(): return lax.all_to_all(array, axis, 0, 0, axis_index_groups=members)]
    unnamed x20 -> x18, local copies, waits for them, and re-layouts: 3.17 us -> 2.38 us
  transfers between devices with their start and end apart: 9 -> 11, of which waited for: 7 -> 7; matrix products, arithmetic and copies ran while one was open for 0% -> 0% of each run, Pallas kernels for 5% -> 7%
where the time goes in v2:
time: 119 us; the launch traced here: 118 us
  starting transfers between devices  42.9 us (36%)
  blocking collectives  35.5 us (30%)
  waiting for transfers between devices  23.3 us (20%)
  Pallas kernels  13.2 us (11%)
  local copies, waits for them, and re-layouts  2.38 us (2%)
    ppermute x4, starting transfers between devices, along_z(): return lax.ppermute(array, 'dp', route)  23.6 us
    all_to_all x1, blocking collectives, spread(): return lax.all_to_all(array, axis, 0, 0, axis_index_groups=members)  20.9 us
    all_to_all x1, blocking collectives, on_device(): squares = lax.all_to_all(squares, 'tensor', 0, 0)  14.6 us
    ppermute x1, waiting for transfers between devices, on_device(): moved = lax.ppermute(moved, 'pipe', onward)  11.9 us
    ppermute x3, starting transfers between devices, along_x(): return lax.ppermute(array, 'pipe', route)  8.91 us
    ppermute x3, waiting for transfers between devices, along_x(): return lax.ppermute(array, 'pipe', route)  5.95 us
    ppermute x4, waiting for transfers between devices, along_z(): return lax.ppermute(array, 'dp', route)  5.44 us
    all_to_all x1, starting transfers between devices, spread(): return lax.all_to_all(array, axis, 0, 0, axis_index_groups=members)  4.5 us
  transfers between devices with their start and end apart: 11, of which 7 were waited for; matrix products, arithmetic and copies ran while one was open for 0% of the time, Pallas kernels for 7%

profile of v2, /device:TPU:6, one launch (start us, length us, event | category | flops | bytes accessed | tf_op | source)
XLA Modules:
  0.0 118.0 jit_solution(8732431133217094315)
XLA Ops:
  0.6 0.0 copy-start.2
  0.7 3.3 %take_moved.1 = f32[3,256,512]{2,1,0:T(8,128)} custom-call(s32[1]{0:T(128)} %bitcast.pos, s32[97]{0:T(128)} %old_starts.7, s32[97]{0:T(128)} %new_starts.7, f32[384,512]{1,0:T(8,128)} %refs_0_.3, f32[384,512]{1,0:T(8,128)} %refs_1_.3, f32[384,512]{1,0:T(8,128)} %refs_2_.3), custom_call_target="tpu_custom_call" | custom-call | bytes 1024 | tf_op jit(solution)/shard_map/take_moved/pallas_call | solution.py:83
  4.0 0.0 copy-start
  4.0 0.0 copy-start.1
  4.0 2.1 %collective-permute-start = (f32[3,256,512]{2,1,0:T(8,128)}, f32[3,256,512]{2,1,0:T(8,128)S(1)}, u32[]{:S(2)}, u32[]{:S(2)}) collective-permute-start(f32[3,256,512]{2,1,0:T(8,128)} %take_moved.1), channel_id=1, source_target_pairs={{0,1},{1,2},{2,3},{4,5},{5,6},{6,7},{8,9},{9,10},{10,11},{12,13},{... | collective-permute-start | bytes 4718600 | tf_op jit(solution)/shard_map/ppermute | solution.py:392
  6.0 0.0 copy-start.3
  6.0 1.4 %copy-done.3 = bf16[256,3072]{1,0:T(8,128)(2,1)S(1)} copy-done((bf16[256,3072]{1,0:T(8,128)(2,1)S(1)}, bf16[256,3072]{1,0:T(8,128)(2,1)}, u32[]{:S(2)}) %copy-start.3) | copy-done | bytes 1572888
  7.4 0.0 copy-start.6
  7.4 0.0 copy-start.7
  7.4 3.0 %turn_hidden.1 = (bf16[3,4,4,32,256]{4,3,2,1,0:T(8,128)(2,1)S(1)}, f32[3,4,4,32,256]{4,3,2,1,0:T(8,128)S(1)}) custom-call(s32[1]{0:T(128)} %bitcast.pos, bf16[256,3072]{1,0:T(8,128)(2,1)S(1)} %copy-done.3), custom_call_target="tpu_custom_call" | custom-call | bytes 1024 | tf_op jit(solution)/shard_map/turn_hidden/pallas_call | solution.py:156
  10.5 1.9 %collective-permute-start.1 = (f32[3,4,4,32,256]{4,3,2,1,0:T(8,128)S(1)}, f32[3,4,4,32,256]{4,3,2,1,0:T(8,128)S(1)}, u32[]{:S(2)}, u32[]{:S(2)}) collective-permute-start(f32[3,4,4,32,256]{4,3,2,1,0:T(8,128)S(1)} %get-tuple-element.37), channel_id=1, source_target_pairs={{0,1},{1,0},{2,3},{3,2},{4,5},{5,4},{6,7},{7,6},{8,9},{9,8},{10,11... | collective-permute-start | bytes 4718600 | tf_op jit(solution)/shard_map/ppermute | solution.py:394
  12.4 0.0 copy-done.2
  12.4 0.0 copy-done
  12.4 0.0 copy-done.1
  12.4 0.0 copy-done.6
  12.5 0.0 copy-done.7
  12.5 0.0 copy-start.4
  12.5 0.9 copy-done.4
  13.4 0.8 keep_own.1.kept
  14.2 11.9 %collective-permute-done.moved = f32[3,256,512]{2,1,0:T(8,128)S(1)} collective-permute-done((f32[3,256,512]{2,1,0:T(8,128)}, f32[3,256,512]{2,1,0:T(8,128)S(1)}, u32[]{:S(2)}, u32[]{:S(2)}) %collective-permute-start) | collective-permute-done | bytes 1572896 | tf_op jit(solution)/shard_map/ppermute | solution.py:392
  26.1 1.0 adam_step.3.weight_mine
  27.1 1.9 %collective-permute-start.2 = (f32[256,512]{1,0:T(8,128)S(1)}, f32[256,512]{1,0:T(8,128)S(1)}, u32[]{:S(2)}, u32[]{:S(2)}) collective-permute-start(f32[256,512]{1,0:T(8,128)S(1)} %adam_step.3.weight_mine), channel_id=1, source_target_pairs={{0,1},{1,0},{2,3},{3,2},{4,5},{5,4},{6,7},{7,6},{8,9},{9,8},{10,11... | collective-permute-start | bytes 1572872 | tf_op jit(solution)/shard_map/ppermute | solution.py:400
  29.0 2.2 %adam_step.2 = (f32[256,512]{1,0:T(8,128)}, f32[256,512]{1,0:T(8,128)}, f32[256,512]{1,0:T(8,128)}) custom-call(s32[1]{0:T(128)} %bitcast.pos, s32[97]{0:T(128)S(1)} %copy-done.6, s32[97]{0:T(128)S(1)} %copy-done.7, f32[4,256,512]{2,1,0:T(8,128)S(1)} %keep_own.1.kept, f32[3,256,512]{2,1,0:T(8,128)S(1)} %collective-permute-done.moved), custom_call_target="tpu_custom_call" | custom-call | bytes 1024 | tf_op jit(solution)/shard_map/adam_step/pallas_call | solution.py:197
  31.2 0.0 collective-permute-done.1
  31.2 0.0 collective-permute-done.2.weight_theirs
  31.2 1.0 products.1
  32.2 4.0 %collective-permute-start.8 = (f32[4,128,256]{2,1,0:T(8,128)S(1)}, f32[4,128,256]{2,1,0:T(8,128)S(1)}, u32[]{:S(2)}, u32[]{:S(2)}) collective-permute-start(f32[4,128,256]{2,1,0:T(8,128)S(1)} %get-tuple-element.46), channel_id=1, source_target_pairs={{0,64},{64,128},{128,192},{192,256},{256,320},{320,384},{384,448},... | collective-permute-start | bytes 1572872 | tf_op jit(solution)/shard_map/ppermute | solution.py:388
  36.3 12.5 %collective-permute-start.9 = (f32[4,128,256]{2,1,0:T(8,128)S(1)}, f32[4,128,256]{2,1,0:T(8,128)S(1)}, u32[]{:S(2)}, u32[]{:S(2)}) collective-permute-start(f32[4,128,256]{2,1,0:T(8,128)S(1)} %get-tuple-element.47), channel_id=1, source_target_pairs={{0,704},{64,0},{128,64},{192,128},{256,192},{320,256},{384,320},{4... | collective-permute-start | bytes 1572872 | tf_op jit(solution)/shard_map/ppermute | solution.py:388
  48.7 3.1 %collective-permute-start.3 = (f32[384,256]{1,0:T(8,128)S(1)}, f32[384,256]{1,0:T(8,128)S(1)}, u32[]{:S(2)}, u32[]{:S(2)}) collective-permute-start(f32[384,256]{1,0:T(8,128)S(1)} %get-tuple-element.39), channel_id=1, source_target_pairs={{0,4},{1,5},{2,6},{3,7},{4,0},{5,1},{6,2},{7,3},{8,12},{9,13},{10,... | collective-permute-start | bytes 1179656 | tf_op jit(solution)/shard_map/ppermute | solution.py:378
  51.8 3.2 %collective-permute-start.4 = (f32[384,256]{1,0:T(8,128)S(1)}, f32[384,256]{1,0:T(8,128)S(1)}, u32[]{:S(2)}, u32[]{:S(2)}) collective-permute-start(f32[384,256]{1,0:T(8,128)S(1)} %get-tuple-element.40), channel_id=1, source_target_pairs={{0,2},{1,3},{2,4},{3,5},{4,6},{5,7},{6,0},{7,1},{8,10},{9,11},{10,... | collective-permute-start | bytes 1179656 | tf_op jit(solution)/shard_map/ppermute | solution.py:378
  55.0 2.7 %collective-permute-start.5 = (f32[384,256]{1,0:T(8,128)S(1)}, f32[384,256]{1,0:T(8,128)S(1)}, u32[]{:S(2)}, u32[]{:S(2)}) collective-permute-start(f32[384,256]{1,0:T(8,128)S(1)} %get-tuple-element.41), channel_id=1, source_target_pairs={{0,6},{1,7},{2,0},{3,1},{4,2},{5,3},{6,4},{7,5},{8,14},{9,15},{10,... | collective-permute-start | bytes 1179656 | tf_op jit(solution)/shard_map/ppermute | solution.py:378
  57.7 1.7 %collective-permute-done.8.refs_1_ = f32[4,128,256]{2,1,0:T(8,128)S(1)} collective-permute-done((f32[4,128,256]{2,1,0:T(8,128)S(1)}, f32[4,128,256]{2,1,0:T(8,128)S(1)}, u32[]{:S(2)}, u32[]{:S(2)}) %collective-permute-start.8) | collective-permute-done | bytes 524320 | tf_op jit(solution)/shard_map/ppermute | solution.py:388
  59.4 1.2 %collective-permute-done.9.refs_2_ = f32[4,128,256]{2,1,0:T(8,128)S(1)} collective-permute-done((f32[4,128,256]{2,1,0:T(8,128)S(1)}, f32[4,128,256]{2,1,0:T(8,128)S(1)}, u32[]{:S(2)}, u32[]{:S(2)}) %collective-permute-start.9) | collective-permute-done | bytes 524320 | tf_op jit(solution)/shard_map/ppermute | solution.py:388
  60.6 0.9 add_up.1
  61.4 4.5 %all-to-all-start = ((f32[4,128,256]{2,1,0:T(8,128)}), f32[4,128,256]{2,1,0:T(8,128)S(1)}, u32[]{:S(2)}, u32[]{:S(2)}) async-start(f32[4,128,256]{2,1,0:T(8,128)} %add_up.1), calls=%async_computation | async-start | bytes 1048576 | tf_op jit(solution)/shard_map/all_to_all | solution.py:384
  65.9 0.0 collective-permute-done.3.refs_1_
  66.0 3.2 %collective-permute-done.4.refs_2_ = f32[384,256]{1,0:T(8,128)S(1)} collective-permute-done((f32[384,256]{1,0:T(8,128)S(1)}, f32[384,256]{1,0:T(8,128)S(1)}, u32[]{:S(2)}, u32[]{:S(2)}) %collective-permute-start.4) | collective-permute-done | bytes 393248 | tf_op jit(solution)/shard_map/ppermute | solution.py:378
  69.2 2.7 %collective-permute-done.5.refs_3_ = f32[384,256]{1,0:T(8,128)S(1)} collective-permute-done((f32[384,256]{1,0:T(8,128)S(1)}, f32[384,256]{1,0:T(8,128)S(1)}, u32[]{:S(2)}, u32[]{:S(2)}) %collective-permute-start.5) | collective-permute-done | bytes 393248 | tf_op jit(solution)/shard_map/ppermute | solution.py:378
  71.9 0.0 copy-start.5
  71.9 0.0 copy-start.8
  71.9 0.1 add_and_split.1
  72.0 1.9 %collective-permute-start.6 = (f32[128,256]{1,0:T(8,128)S(1)}, f32[128,256]{1,0:T(8,128)S(1)}, u32[]{:S(2)}, u32[]{:S(2)}) collective-permute-start(f32[128,256]{1,0:T(8,128)S(1)} %get-tuple-element.43), channel_id=1, source_target_pairs={{0,64},{64,128},{128,192},{192,256},{256,320},{320,384},{384,448},... | collective-permute-start | bytes 393224 | tf_op jit(solution)/shard_map/ppermute | solution.py:388
  73.9 5.1 %collective-permute-start.7 = (f32[128,256]{1,0:T(8,128)S(1)}, f32[128,256]{1,0:T(8,128)S(1)}, u32[]{:S(2)}, u32[]{:S(2)}) collective-permute-start(f32[128,256]{1,0:T(8,128)S(1)} %get-tuple-element.44), channel_id=1, source_target_pairs={{0,704},{64,0},{128,64},{192,128},{256,192},{320,256},{384,320},{4... | collective-permute-start | bytes 393224 | tf_op jit(solution)/shard_map/ppermute | solution.py:388
  79.0 1.4 %collective-permute-done.6.refs_1_ = f32[128,256]{1,0:T(8,128)S(1)} collective-permute-done((f32[128,256]{1,0:T(8,128)S(1)}, f32[128,256]{1,0:T(8,128)S(1)}, u32[]{:S(2)}, u32[]{:S(2)}) %collective-permute-start.6) | collective-permute-done | bytes 131104 | tf_op jit(solution)/shard_map/ppermute | solution.py:388
  80.4 1.2 %collective-permute-done.7.refs_2_ = f32[128,256]{1,0:T(8,128)S(1)} collective-permute-done((f32[128,256]{1,0:T(8,128)S(1)}, f32[128,256]{1,0:T(8,128)S(1)}, u32[]{:S(2)}, u32[]{:S(2)}) %collective-permute-start.7) | collective-permute-done | bytes 131104 | tf_op jit(solution)/shard_map/ppermute | solution.py:388
  81.6 0.0 all-to-all-done.refs_3_
  81.6 20.9 %all_to_all.15.parts = f32[4,32,512]{2,1,0:T(8,128)S(1)} all-to-all(f32[4,32,512]{2,1,0:T(8,128)S(1)} %add_and_merge.1), channel_id=1, replica_groups={{0,192,384,576},{64,256,448,640},{128,320,512,704},{1,193,385,577},{65,..., dimensions={0} | all-to-all | bytes 524288 | tf_op jit(solution)/shard_map/all_to_all | solution.py:384
  102.6 0.0 copy-done.5
  102.6 0.2 total_up.1
  102.8 14.6 %all_to_all.16.squares = f32[8,1,128]{2,1,0:T(1,128)S(1)} all-to-all(f32[8,1,128]{2,1,0:T(1,128)S(1)} %get-tuple-element.49), channel_id=1, replica_groups=mesh['dp'=12,'tensor'=8,'pipe'=8] {'tensor'}, dimensions={0} | all-to-all | bytes 8192 | tf_op jit(solution)/shard_map/all_to_all | solution.py:411
  117.3 0.0 copy-done.8
  117.3 0.7 finish.1
  (1 shorter events, 0.0 us)
Async XLA Ops:
  0.6 11.8 %copy-start.2 = (f32[384,512]{1,0:T(8,128)S(1)}, f32[384,512]{1,0:T(8,128)}, u32[]{:S(2)}) copy-start(f32[384,512]{1,0:T(8,128)} %refs_2_.3) | copy-start | bytes 2359300
  4.0 8.5 %copy-start = (f32[384,512]{1,0:T(8,128)S(1)}, f32[384,512]{1,0:T(8,128)}, u32[]{:S(2)}) copy-start(f32[384,512]{1,0:T(8,128)} %refs_0_.3) | copy-start | bytes 2359300
  4.0 8.5 %copy-start.1 = (f32[384,512]{1,0:T(8,128)S(1)}, f32[384,512]{1,0:T(8,128)}, u32[]{:S(2)}) copy-start(f32[384,512]{1,0:T(8,128)} %refs_1_.3) | copy-start | bytes 2359300
  4.0 22.1 %collective-permute-start = (f32[3,256,512]{2,1,0:T(8,128)}, f32[3,256,512]{2,1,0:T(8,128)S(1)}, u32[]{:S(2)}, u32[]{:S(2)}) collective-permute-start(f32[3,256,512]{2,1,0:T(8,128)} %take_moved.1), channel_id=1, source_target_pairs={{0,1},{1,2},{2,3},{4,5},{5,6},{6,7},{8,9},{9,10},{10,11},{12,13},{... | collective-permute-start | bytes 4718600 | tf_op jit(solution)/shard_map/ppermute | solution.py:392
  6.0 1.4 %copy-start.3 = (bf16[256,3072]{1,0:T(8,128)(2,1)S(1)}, bf16[256,3072]{1,0:T(8,128)(2,1)}, u32[]{:S(2)}) copy-start(bf16[256,3072]{1,0:T(8,128)(2,1)} %block.1) | copy-start | bytes 4718596
  7.4 5.0 %copy-start.6 = (s32[97]{0:T(128)S(1)}, s32[97]{0:T(128)}, u32[]{:S(2)}) copy-start(s32[97]{0:T(128)} %old_starts.7) | copy-start | bytes 1168
  7.4 5.0 %copy-start.7 = (s32[97]{0:T(128)S(1)}, s32[97]{0:T(128)}, u32[]{:S(2)}) copy-start(s32[97]{0:T(128)} %new_starts.7) | copy-start | bytes 1168
  10.5 20.7 %collective-permute-start.1 = (f32[3,4,4,32,256]{4,3,2,1,0:T(8,128)S(1)}, f32[3,4,4,32,256]{4,3,2,1,0:T(8,128)S(1)}, u32[]{:S(2)}, u32[]{:S(2)}) collective-permute-start(f32[3,4,4,32,256]{4,3,2,1,0:T(8,128)S(1)} %get-tuple-element.37), channel_id=1, source_target_pairs={{0,1},{1,0},{2,3},{3,2},{4,5},{5,4},{6,7},{7,6},{8,9},{9,8},{10,11... | collective-permute-start | bytes 4718600 | tf_op jit(solution)/shard_map/ppermute | solution.py:394
  12.5 1.0 copy-start.4
  27.1 4.1 %collective-permute-start.2 = (f32[256,512]{1,0:T(8,128)S(1)}, f32[256,512]{1,0:T(8,128)S(1)}, u32[]{:S(2)}, u32[]{:S(2)}) collective-permute-start(f32[256,512]{1,0:T(8,128)S(1)} %adam_step.3.weight_mine), channel_id=1, source_target_pairs={{0,1},{1,0},{2,3},{3,2},{4,5},{5,4},{6,7},{7,6},{8,9},{9,8},{10,11... | collective-permute-start | bytes 1572872 | tf_op jit(solution)/shard_map/ppermute | solution.py:400
  32.2 27.2 %collective-permute-start.8 = (f32[4,128,256]{2,1,0:T(8,128)S(1)}, f32[4,128,256]{2,1,0:T(8,128)S(1)}, u32[]{:S(2)}, u32[]{:S(2)}) collective-permute-start(f32[4,128,256]{2,1,0:T(8,128)S(1)} %get-tuple-element.46), channel_id=1, source_target_pairs={{0,64},{64,128},{128,192},{192,256},{256,320},{320,384},{384,448},... | collective-permute-start | bytes 1572872 | tf_op jit(solution)/shard_map/ppermute | solution.py:388
  36.3 24.3 %collective-permute-start.9 = (f32[4,128,256]{2,1,0:T(8,128)S(1)}, f32[4,128,256]{2,1,0:T(8,128)S(1)}, u32[]{:S(2)}, u32[]{:S(2)}) collective-permute-start(f32[4,128,256]{2,1,0:T(8,128)S(1)} %get-tuple-element.47), channel_id=1, source_target_pairs={{0,704},{64,0},{128,64},{192,128},{256,192},{320,256},{384,320},{4... | collective-permute-start | bytes 1572872 | tf_op jit(solution)/shard_map/ppermute | solution.py:388
  48.7 17.2 %collective-permute-start.3 = (f32[384,256]{1,0:T(8,128)S(1)}, f32[384,256]{1,0:T(8,128)S(1)}, u32[]{:S(2)}, u32[]{:S(2)}) collective-permute-start(f32[384,256]{1,0:T(8,128)S(1)} %get-tuple-element.39), channel_id=1, source_target_pairs={{0,4},{1,5},{2,6},{3,7},{4,0},{5,1},{6,2},{7,3},{8,12},{9,13},{10,... | collective-permute-start | bytes 1179656 | tf_op jit(solution)/shard_map/ppermute | solution.py:378
  51.8 17.4 %collective-permute-start.4 = (f32[384,256]{1,0:T(8,128)S(1)}, f32[384,256]{1,0:T(8,128)S(1)}, u32[]{:S(2)}, u32[]{:S(2)}) collective-permute-start(f32[384,256]{1,0:T(8,128)S(1)} %get-tuple-element.40), channel_id=1, source_target_pairs={{0,2},{1,3},{2,4},{3,5},{4,6},{5,7},{6,0},{7,1},{8,10},{9,11},{10,... | collective-permute-start | bytes 1179656 | tf_op jit(solution)/shard_map/ppermute | solution.py:378
  55.0 16.9 %collective-permute-start.5 = (f32[384,256]{1,0:T(8,128)S(1)}, f32[384,256]{1,0:T(8,128)S(1)}, u32[]{:S(2)}, u32[]{:S(2)}) collective-permute-start(f32[384,256]{1,0:T(8,128)S(1)} %get-tuple-element.41), channel_id=1, source_target_pairs={{0,6},{1,7},{2,0},{3,1},{4,2},{5,3},{6,4},{7,5},{8,14},{9,15},{10,... | collective-permute-start | bytes 1179656 | tf_op jit(solution)/shard_map/ppermute | solution.py:378
  61.4 20.1 %all-to-all-start = ((f32[4,128,256]{2,1,0:T(8,128)}), f32[4,128,256]{2,1,0:T(8,128)S(1)}, u32[]{:S(2)}, u32[]{:S(2)}) async-start(f32[4,128,256]{2,1,0:T(8,128)} %add_up.1), calls=%async_computation | async-start | bytes 1048576 | tf_op jit(solution)/shard_map/all_to_all | solution.py:384
  71.9 30.7 %copy-start.5 = (bf16[32,512]{1,0:T(8,128)(2,1)S(1)}, bf16[32,512]{1,0:T(8,128)(2,1)}, u32[]{:S(2)}) copy-start(bf16[32,512]{1,0:T(8,128)(2,1)} %residual.1) | copy-start | bytes 98308
  71.9 45.4 %copy-start.8 = (f32[512]{0:T(512)S(1)}, f32[512]{0:T(512)}, u32[]{:S(2)}) copy-start(f32[512]{0:T(512)} %param.15) | copy-start | bytes 6148
  72.0 8.4 %collective-permute-start.6 = (f32[128,256]{1,0:T(8,128)S(1)}, f32[128,256]{1,0:T(8,128)S(1)}, u32[]{:S(2)}, u32[]{:S(2)}) collective-permute-start(f32[128,256]{1,0:T(8,128)S(1)} %get-tuple-element.43), channel_id=1, source_target_pairs={{0,64},{64,128},{128,192},{192,256},{256,320},{320,384},{384,448},... | collective-permute-start | bytes 393224 | tf_op jit(solution)/shard_map/ppermute | solution.py:388
  73.9 7.7 %collective-permute-start.7 = (f32[128,256]{1,0:T(8,128)S(1)}, f32[128,256]{1,0:T(8,128)S(1)}, u32[]{:S(2)}, u32[]{:S(2)}) collective-permute-start(f32[128,256]{1,0:T(8,128)S(1)} %get-tuple-element.44), channel_id=1, source_target_pairs={{0,704},{64,0},{128,64},{192,128},{256,192},{320,256},{384,320},{4... | collective-permute-start | bytes 393224 | tf_op jit(solution)/shard_map/ppermute | solution.py:388

commit v3 on v2

--- a/solution.py
+++ b/solution.py
@@ -169,7 +169,7 @@
     )(pos, hidden)
 
 
-def adam_kernel(pos, old_starts, new_starts, kept, moved, new_weight, *moments):
+def adam_kernel(pos, old_starts, new_starts, kept, moved, *refs):
     here = pos[0]
     for lane in range(2):
         block = new_starts[here] + lane
@@ -184,25 +184,28 @@
         grad = kept[3, rows, :]
         first_new = decay_first * first_old + (1.0 - decay_first) * grad
         second_new = decay_second * second_old + (1.0 - decay_second) * grad * grad
+        if len(refs) > 1:
+            sent, new_weight, new_first, new_second = refs
+            new_weight[rows, :] = sent[rows, :]
+            new_first[rows, :] = jnp.where(live, first_new, 0.0)
+            new_second[rows, :] = jnp.where(live, second_new, 0.0)
+            continue
         step_dir = (first_new / corr_first) / (jnp.sqrt(second_new / corr_second) + adam_eps)
         weight_next = weight_old - learn_rate * (step_dir + weight_decay * weight_old)
-        new_weight[rows, :] = jnp.where(live, weight_next, 0.0)
-        if moments:
-            new_first, new_second = moments
-            new_first[rows, :] = jnp.where(live, first_new, 0.0)
-            new_second[rows, :] = jnp.where(live, second_new, 0.0)
-
-
-def adam_step(scalars, kept, moved, count):
+        refs[0][rows, :] = jnp.where(live, weight_next, 0.0)
+
+
+def adam_step(scalars, kept, moved, *sent):
+    count = 3 if sent else 1
     return pl.pallas_call(
         adam_kernel,
         in_specs=[pl.BlockSpec(memory_space=pltpu.SMEM)] * 3
-        + [pl.BlockSpec(memory_space=pltpu.VMEM)] * 2,
+        + [pl.BlockSpec(memory_space=pltpu.VMEM)] * (2 + len(sent)),
         out_shape=[jax.ShapeDtypeStruct(kept.shape[1:], F32)] * count,
         compiler_params=params(),
         cost_estimate=COST,
         name="adam_step",
-    )(*scalars, kept, moved)
+    )(*scalars, kept, moved, *sent)
 
 
 def product_kernel(mine, theirs, weight_mine, weight_theirs, *outs):
@@ -396,9 +399,9 @@
     theirs = theirs.reshape(3, seats, hops * SEAT, depth)
     kept = keep_own((after, old_starts, new_starts), olds, gradient)
 
-    (sent,) = adam_step(scalars, kept, moved, 1)
+    (sent,) = adam_step(scalars, kept, moved)
     received = lax.ppermute(sent, "pipe", across)
-    state = adam_step(scalars, kept, moved, 3)
+    state = adam_step(scalars, kept, moved, sent)
     mine, *state = lax.optimization_barrier((mine, *state))
     *half_a, first_b, plus_b, minus_b = products(mine, theirs, sent, received)
     plus_b, minus_b = along_z(plus_b, 1), along_z(minus_b, -1)

time: 119 us -> 118 us (level)
  no operation moved by 1% of the time
where the time goes in v3:
time: 118 us
  starting transfers between devices  43.2 us (37%)
  blocking collectives  35.5 us (30%)
  waiting for transfers between devices  23.2 us (20%)
  Pallas kernels  12.7 us (11%)
  local copies, waits for them, and re-layouts  2.38 us (2%)
    ppermute x4, starting transfers between devices, along_z(): return lax.ppermute(array, 'dp', route)  23.8 us
    all_to_all x1, blocking collectives, spread(): return lax.all_to_all(array, axis, 0, 0, axis_index_groups=members)  20.9 us
    all_to_all x1, blocking collectives, on_device(): squares = lax.all_to_all(squares, 'tensor', 0, 0)  14.6 us
    ppermute x1, waiting for transfers between devices, on_device(): moved = lax.ppermute(moved, 'pipe', onward)  11.8 us
    ppermute x3, starting transfers between devices, along_x(): return lax.ppermute(array, 'pipe', route)  8.91 us
    ppermute x3, waiting for transfers between devices, along_x(): return lax.ppermute(array, 'pipe', route)  5.95 us
    ppermute x4, waiting for transfers between devices, along_z(): return lax.ppermute(array, 'dp', route)  5.44 us
    all_to_all x1, starting transfers between devices, spread(): return lax.all_to_all(array, axis, 0, 0, axis_index_groups=members)  4.5 us
  transfers between devices with their start and end apart: 11, of which 7 were waited for; matrix products, arithmetic and copies ran while one was open for 0% of the time, Pallas kernels for 7%

profile of v3, /device:TPU:6, one launch (start us, length us, event | category | flops | bytes accessed | tf_op | source)
XLA Modules:
  0.0 117.8 jit_solution(6059969310102429536)
XLA Ops:
  0.6 0.0 copy-start.2
  0.7 3.0 %take_moved.1 = f32[3,256,512]{2,1,0:T(8,128)} custom-call(s32[1]{0:T(128)} %bitcast.pos, s32[97]{0:T(128)} %old_starts.7, s32[97]{0:T(128)} %new_starts.7, f32[384,512]{1,0:T(8,128)} %refs_0_.3, f32[384,512]{1,0:T(8,128)} %refs_1_.3, f32[384,512]{1,0:T(8,128)} %refs_2_.3), custom_call_target="tpu_custom_call" | custom-call | bytes 1024 | tf_op jit(solution)/shard_map/take_moved/pallas_call | solution.py:83
  3.7 0.0 copy-start
  3.7 0.0 copy-start.1
  3.7 2.1 %collective-permute-start = (f32[3,256,512]{2,1,0:T(8,128)}, f32[3,256,512]{2,1,0:T(8,128)S(1)}, u32[]{:S(2)}, u32[]{:S(2)}) collective-permute-start(f32[3,256,512]{2,1,0:T(8,128)} %take_moved.1), channel_id=1, source_target_pairs={{0,1},{1,2},{2,3},{4,5},{5,6},{6,7},{8,9},{9,10},{10,11},{12,13},{... | collective-permute-start | bytes 4718600 | tf_op jit(solution)/shard_map/ppermute | solution.py:395
  5.9 0.0 copy-start.3
  5.9 1.4 %copy-done.3 = bf16[256,3072]{1,0:T(8,128)(2,1)S(1)} copy-done((bf16[256,3072]{1,0:T(8,128)(2,1)S(1)}, bf16[256,3072]{1,0:T(8,128)(2,1)}, u32[]{:S(2)}) %copy-start.3) | copy-done | bytes 1572888
  7.3 0.0 copy-start.6
  7.3 0.0 copy-start.7
  7.3 3.0 %turn_hidden.1 = (bf16[3,4,4,32,256]{4,3,2,1,0:T(8,128)(2,1)S(1)}, f32[3,4,4,32,256]{4,3,2,1,0:T(8,128)S(1)}) custom-call(s32[1]{0:T(128)} %bitcast.pos, bf16[256,3072]{1,0:T(8,128)(2,1)S(1)} %copy-done.3), custom_call_target="tpu_custom_call" | custom-call | bytes 1024 | tf_op jit(solution)/shard_map/turn_hidden/pallas_call | solution.py:156
  10.3 1.9 %collective-permute-start.1 = (f32[3,4,4,32,256]{4,3,2,1,0:T(8,128)S(1)}, f32[3,4,4,32,256]{4,3,2,1,0:T(8,128)S(1)}, u32[]{:S(2)}, u32[]{:S(2)}) collective-permute-start(f32[3,4,4,32,256]{4,3,2,1,0:T(8,128)S(1)} %get-tuple-element.37), channel_id=1, source_target_pairs={{0,1},{1,0},{2,3},{3,2},{4,5},{5,4},{6,7},{7,6},{8,9},{9,8},{10,11... | collective-permute-start | bytes 4718600 | tf_op jit(solution)/shard_map/ppermute | solution.py:397
  12.2 0.0 copy-done.2
  12.2 0.0 copy-done
  12.3 0.0 copy-done.1
  12.3 0.0 copy-done.6
  12.3 0.0 copy-done.7
  12.3 0.0 copy-start.4
  12.3 0.9 copy-done.4
  13.2 0.8 keep_own.1.kept
  14.0 11.8 %collective-permute-done.moved = f32[3,256,512]{2,1,0:T(8,128)S(1)} collective-permute-done((f32[3,256,512]{2,1,0:T(8,128)}, f32[3,256,512]{2,1,0:T(8,128)S(1)}, u32[]{:S(2)}, u32[]{:S(2)}) %collective-permute-start) | collective-permute-done | bytes 1572896 | tf_op jit(solution)/shard_map/ppermute | solution.py:395
  25.8 1.0 adam_step.2.refs_0_.weight_mine
  26.8 1.9 %collective-permute-start.2 = (f32[256,512]{1,0:T(8,128)S(1)}, f32[256,512]{1,0:T(8,128)S(1)}, u32[]{:S(2)}, u32[]{:S(2)}) collective-permute-start(f32[256,512]{1,0:T(8,128)S(1)} %adam_step.2.refs_0_.weight_mine), channel_id=1, source_target_pairs={{0,1},{1,0},{2,3},{3,2},{4,5},{5,4},{6,7},{7,6},{8,9},{9,8},{10,11... | collective-permute-start | bytes 1572872 | tf_op jit(solution)/shard_map/ppermute | solution.py:403
  28.8 1.9 %adam_step.3 = (f32[256,512]{1,0:T(8,128)}, f32[256,512]{1,0:T(8,128)}, f32[256,512]{1,0:T(8,128)}) custom-call(s32[1]{0:T(128)} %bitcast.pos, s32[97]{0:T(128)S(1)} %copy-done.6, s32[97]{0:T(128)S(1)} %copy-done.7, f32[4,256,512]{2,1,0:T(8,128)S(1)} %keep_own.1.kept, f32[3,256,512]{2,1,0:T(8,128)S(1)} %collective-permute-done.moved, ...), custom_call_target="tpu_custom_call" | custom-call | bytes 1024 | tf_op jit(solution)/shard_map/adam_step/pallas_call | solution.py:200
  30.7 0.0 collective-permute-done.1
  30.7 0.0 collective-permute-done.2.weight_theirs
  30.7 1.0 products.1
  31.7 4.3 %collective-permute-start.8 = (f32[4,128,256]{2,1,0:T(8,128)S(1)}, f32[4,128,256]{2,1,0:T(8,128)S(1)}, u32[]{:S(2)}, u32[]{:S(2)}) collective-permute-start(f32[4,128,256]{2,1,0:T(8,128)S(1)} %get-tuple-element.46), channel_id=1, source_target_pairs={{0,64},{64,128},{128,192},{192,256},{256,320},{320,384},{384,448},... | collective-permute-start | bytes 1572872 | tf_op jit(solution)/shard_map/ppermute | solution.py:391
  36.0 12.5 %collective-permute-start.9 = (f32[4,128,256]{2,1,0:T(8,128)S(1)}, f32[4,128,256]{2,1,0:T(8,128)S(1)}, u32[]{:S(2)}, u32[]{:S(2)}) collective-permute-start(f32[4,128,256]{2,1,0:T(8,128)S(1)} %get-tuple-element.47), channel_id=1, source_target_pairs={{0,704},{64,0},{128,64},{192,128},{256,192},{320,256},{384,320},{4... | collective-permute-start | bytes 1572872 | tf_op jit(solution)/shard_map/ppermute | solution.py:391
  48.5 3.1 %collective-permute-start.3 = (f32[384,256]{1,0:T(8,128)S(1)}, f32[384,256]{1,0:T(8,128)S(1)}, u32[]{:S(2)}, u32[]{:S(2)}) collective-permute-start(f32[384,256]{1,0:T(8,128)S(1)} %get-tuple-element.39), channel_id=1, source_target_pairs={{0,4},{1,5},{2,6},{3,7},{4,0},{5,1},{6,2},{7,3},{8,12},{9,13},{10,... | collective-permute-start | bytes 1179656 | tf_op jit(solution)/shard_map/ppermute | solution.py:381
  51.6 3.2 %collective-permute-start.4 = (f32[384,256]{1,0:T(8,128)S(1)}, f32[384,256]{1,0:T(8,128)S(1)}, u32[]{:S(2)}, u32[]{:S(2)}) collective-permute-start(f32[384,256]{1,0:T(8,128)S(1)} %get-tuple-element.40), channel_id=1, source_target_pairs={{0,2},{1,3},{2,4},{3,5},{4,6},{5,7},{6,0},{7,1},{8,10},{9,11},{10,... | collective-permute-start | bytes 1179656 | tf_op jit(solution)/shard_map/ppermute | solution.py:381
  54.8 2.7 %collective-permute-start.5 = (f32[384,256]{1,0:T(8,128)S(1)}, f32[384,256]{1,0:T(8,128)S(1)}, u32[]{:S(2)}, u32[]{:S(2)}) collective-permute-start(f32[384,256]{1,0:T(8,128)S(1)} %get-tuple-element.41), channel_id=1, source_target_pairs={{0,6},{1,7},{2,0},{3,1},{4,2},{5,3},{6,4},{7,5},{8,14},{9,15},{10,... | collective-permute-start | bytes 1179656 | tf_op jit(solution)/shard_map/ppermute | solution.py:381
  57.4 1.7 %collective-permute-done.8.refs_1_ = f32[4,128,256]{2,1,0:T(8,128)S(1)} collective-permute-done((f32[4,128,256]{2,1,0:T(8,128)S(1)}, f32[4,128,256]{2,1,0:T(8,128)S(1)}, u32[]{:S(2)}, u32[]{:S(2)}) %collective-permute-start.8) | collective-permute-done | bytes 524320 | tf_op jit(solution)/shard_map/ppermute | solution.py:391
  59.1 1.2 %collective-permute-done.9.refs_2_ = f32[4,128,256]{2,1,0:T(8,128)S(1)} collective-permute-done((f32[4,128,256]{2,1,0:T(8,128)S(1)}, f32[4,128,256]{2,1,0:T(8,128)S(1)}, u32[]{:S(2)}, u32[]{:S(2)}) %collective-permute-start.9) | collective-permute-done | bytes 524320 | tf_op jit(solution)/shard_map/ppermute | solution.py:391
  60.3 0.9 add_up.1
  61.2 4.5 %all-to-all-start = ((f32[4,128,256]{2,1,0:T(8,128)}), f32[4,128,256]{2,1,0:T(8,128)S(1)}, u32[]{:S(2)}, u32[]{:S(2)}) async-start(f32[4,128,256]{2,1,0:T(8,128)} %add_up.1), calls=%async_computation | async-start | bytes 1048576 | tf_op jit(solution)/shard_map/all_to_all | solution.py:387
  65.7 0.0 collective-permute-done.3.refs_1_
  65.7 3.2 %collective-permute-done.4.refs_2_ = f32[384,256]{1,0:T(8,128)S(1)} collective-permute-done((f32[384,256]{1,0:T(8,128)S(1)}, f32[384,256]{1,0:T(8,128)S(1)}, u32[]{:S(2)}, u32[]{:S(2)}) %collective-permute-start.4) | collective-permute-done | bytes 393248 | tf_op jit(solution)/shard_map/ppermute | solution.py:381
  68.9 2.7 %collective-permute-done.5.refs_3_ = f32[384,256]{1,0:T(8,128)S(1)} collective-permute-done((f32[384,256]{1,0:T(8,128)S(1)}, f32[384,256]{1,0:T(8,128)S(1)}, u32[]{:S(2)}, u32[]{:S(2)}) %collective-permute-start.5) | collective-permute-done | bytes 393248 | tf_op jit(solution)/shard_map/ppermute | solution.py:381
  71.7 0.0 copy-start.5
  71.7 0.0 copy-start.8
  71.7 0.1 add_and_split.1
  71.7 1.9 %collective-permute-start.6 = (f32[128,256]{1,0:T(8,128)S(1)}, f32[128,256]{1,0:T(8,128)S(1)}, u32[]{:S(2)}, u32[]{:S(2)}) collective-permute-start(f32[128,256]{1,0:T(8,128)S(1)} %get-tuple-element.43), channel_id=1, source_target_pairs={{0,64},{64,128},{128,192},{192,256},{256,320},{320,384},{384,448},... | collective-permute-start | bytes 393224 | tf_op jit(solution)/shard_map/ppermute | solution.py:391
  73.7 5.1 %collective-permute-start.7 = (f32[128,256]{1,0:T(8,128)S(1)}, f32[128,256]{1,0:T(8,128)S(1)}, u32[]{:S(2)}, u32[]{:S(2)}) collective-permute-start(f32[128,256]{1,0:T(8,128)S(1)} %get-tuple-element.44), channel_id=1, source_target_pairs={{0,704},{64,0},{128,64},{192,128},{256,192},{320,256},{384,320},{4... | collective-permute-start | bytes 393224 | tf_op jit(solution)/shard_map/ppermute | solution.py:391
  78.8 1.4 %collective-permute-done.6.refs_1_ = f32[128,256]{1,0:T(8,128)S(1)} collective-permute-done((f32[128,256]{1,0:T(8,128)S(1)}, f32[128,256]{1,0:T(8,128)S(1)}, u32[]{:S(2)}, u32[]{:S(2)}) %collective-permute-start.6) | collective-permute-done | bytes 131104 | tf_op jit(solution)/shard_map/ppermute | solution.py:391
  80.2 1.2 %collective-permute-done.7.refs_2_ = f32[128,256]{1,0:T(8,128)S(1)} collective-permute-done((f32[128,256]{1,0:T(8,128)S(1)}, f32[128,256]{1,0:T(8,128)S(1)}, u32[]{:S(2)}, u32[]{:S(2)}) %collective-permute-start.7) | collective-permute-done | bytes 131104 | tf_op jit(solution)/shard_map/ppermute | solution.py:391
  81.3 0.0 all-to-all-done.refs_3_
  81.4 20.9 %all_to_all.15.parts = f32[4,32,512]{2,1,0:T(8,128)S(1)} all-to-all(f32[4,32,512]{2,1,0:T(8,128)S(1)} %add_and_merge.1), channel_id=1, replica_groups={{0,192,384,576},{64,256,448,640},{128,320,512,704},{1,193,385,577},{65,..., dimensions={0} | all-to-all | bytes 524288 | tf_op jit(solution)/shard_map/all_to_all | solution.py:387
  102.3 0.0 copy-done.5
  102.3 0.2 total_up.1
  102.5 14.6 %all_to_all.16.squares = f32[8,1,128]{2,1,0:T(1,128)S(1)} all-to-all(f32[8,1,128]{2,1,0:T(1,128)S(1)} %get-tuple-element.49), channel_id=1, replica_groups=mesh['dp'=12,'tensor'=8,'pipe'=8] {'tensor'}, dimensions={0} | all-to-all | bytes 8192 | tf_op jit(solution)/shard_map/all_to_all | solution.py:414
  117.1 0.0 copy-done.8
  117.1 0.7 finish.1
  (1 shorter events, 0.0 us)
Async XLA Ops:
  0.6 11.6 %copy-start.2 = (f32[384,512]{1,0:T(8,128)S(1)}, f32[384,512]{1,0:T(8,128)}, u32[]{:S(2)}) copy-start(f32[384,512]{1,0:T(8,128)} %refs_2_.3) | copy-start | bytes 2359300
  3.7 8.6 %copy-start = (f32[384,512]{1,0:T(8,128)S(1)}, f32[384,512]{1,0:T(8,128)}, u32[]{:S(2)}) copy-start(f32[384,512]{1,0:T(8,128)} %refs_0_.3) | copy-start | bytes 2359300
  3.7 8.5 %copy-start.1 = (f32[384,512]{1,0:T(8,128)S(1)}, f32[384,512]{1,0:T(8,128)}, u32[]{:S(2)}) copy-start(f32[384,512]{1,0:T(8,128)} %refs_1_.3) | copy-start | bytes 2359300
  3.7 22.1 %collective-permute-start = (f32[3,256,512]{2,1,0:T(8,128)}, f32[3,256,512]{2,1,0:T(8,128)S(1)}, u32[]{:S(2)}, u32[]{:S(2)}) collective-permute-start(f32[3,256,512]{2,1,0:T(8,128)} %take_moved.1), channel_id=1, source_target_pairs={{0,1},{1,2},{2,3},{4,5},{5,6},{6,7},{8,9},{9,10},{10,11},{12,13},{... | collective-permute-start | bytes 4718600 | tf_op jit(solution)/shard_map/ppermute | solution.py:395
  5.9 1.4 %copy-start.3 = (bf16[256,3072]{1,0:T(8,128)(2,1)S(1)}, bf16[256,3072]{1,0:T(8,128)(2,1)}, u32[]{:S(2)}) copy-start(bf16[256,3072]{1,0:T(8,128)(2,1)} %block.1) | copy-start | bytes 4718596
  7.3 5.0 %copy-start.6 = (s32[97]{0:T(128)S(1)}, s32[97]{0:T(128)}, u32[]{:S(2)}) copy-start(s32[97]{0:T(128)} %old_starts.7) | copy-start | bytes 1168
  7.3 5.0 %copy-start.7 = (s32[97]{0:T(128)S(1)}, s32[97]{0:T(128)}, u32[]{:S(2)}) copy-start(s32[97]{0:T(128)} %new_starts.7) | copy-start | bytes 1168
  10.3 20.4 %collective-permute-start.1 = (f32[3,4,4,32,256]{4,3,2,1,0:T(8,128)S(1)}, f32[3,4,4,32,256]{4,3,2,1,0:T(8,128)S(1)}, u32[]{:S(2)}, u32[]{:S(2)}) collective-permute-start(f32[3,4,4,32,256]{4,3,2,1,0:T(8,128)S(1)} %get-tuple-element.37), channel_id=1, source_target_pairs={{0,1},{1,0},{2,3},{3,2},{4,5},{5,4},{6,7},{7,6},{8,9},{9,8},{10,11... | collective-permute-start | bytes 4718600 | tf_op jit(solution)/shard_map/ppermute | solution.py:397
  12.3 1.0 copy-start.4
  26.8 3.9 %collective-permute-start.2 = (f32[256,512]{1,0:T(8,128)S(1)}, f32[256,512]{1,0:T(8,128)S(1)}, u32[]{:S(2)}, u32[]{:S(2)}) collective-permute-start(f32[256,512]{1,0:T(8,128)S(1)} %adam_step.2.refs_0_.weight_mine), channel_id=1, source_target_pairs={{0,1},{1,0},{2,3},{3,2},{4,5},{5,4},{6,7},{7,6},{8,9},{9,8},{10,11... | collective-permute-start | bytes 1572872 | tf_op jit(solution)/shard_map/ppermute | solution.py:403
  31.7 27.4 %collective-permute-start.8 = (f32[4,128,256]{2,1,0:T(8,128)S(1)}, f32[4,128,256]{2,1,0:T(8,128)S(1)}, u32[]{:S(2)}, u32[]{:S(2)}) collective-permute-start(f32[4,128,256]{2,1,0:T(8,128)S(1)} %get-tuple-element.46), channel_id=1, source_target_pairs={{0,64},{64,128},{128,192},{192,256},{256,320},{320,384},{384,448},... | collective-permute-start | bytes 1572872 | tf_op jit(solution)/shard_map/ppermute | solution.py:391
  36.0 24.3 %collective-permute-start.9 = (f32[4,128,256]{2,1,0:T(8,128)S(1)}, f32[4,128,256]{2,1,0:T(8,128)S(1)}, u32[]{:S(2)}, u32[]{:S(2)}) collective-permute-start(f32[4,128,256]{2,1,0:T(8,128)S(1)} %get-tuple-element.47), channel_id=1, source_target_pairs={{0,704},{64,0},{128,64},{192,128},{256,192},{320,256},{384,320},{4... | collective-permute-start | bytes 1572872 | tf_op jit(solution)/shard_map/ppermute | solution.py:391
  48.5 17.2 %collective-permute-start.3 = (f32[384,256]{1,0:T(8,128)S(1)}, f32[384,256]{1,0:T(8,128)S(1)}, u32[]{:S(2)}, u32[]{:S(2)}) collective-permute-start(f32[384,256]{1,0:T(8,128)S(1)} %get-tuple-element.39), channel_id=1, source_target_pairs={{0,4},{1,5},{2,6},{3,7},{4,0},{5,1},{6,2},{7,3},{8,12},{9,13},{10,... | collective-permute-start | bytes 1179656 | tf_op jit(solution)/shard_map/ppermute | solution.py:381
  51.6 17.4 %collective-permute-start.4 = (f32[384,256]{1,0:T(8,128)S(1)}, f32[384,256]{1,0:T(8,128)S(1)}, u32[]{:S(2)}, u32[]{:S(2)}) collective-permute-start(f32[384,256]{1,0:T(8,128)S(1)} %get-tuple-element.40), channel_id=1, source_target_pairs={{0,2},{1,3},{2,4},{3,5},{4,6},{5,7},{6,0},{7,1},{8,10},{9,11},{10,... | collective-permute-start | bytes 1179656 | tf_op jit(solution)/shard_map/ppermute | solution.py:381
  54.8 16.9 %collective-permute-start.5 = (f32[384,256]{1,0:T(8,128)S(1)}, f32[384,256]{1,0:T(8,128)S(1)}, u32[]{:S(2)}, u32[]{:S(2)}) collective-permute-start(f32[384,256]{1,0:T(8,128)S(1)} %get-tuple-element.41), channel_id=1, source_target_pairs={{0,6},{1,7},{2,0},{3,1},{4,2},{5,3},{6,4},{7,5},{8,14},{9,15},{10,... | collective-permute-start | bytes 1179656 | tf_op jit(solution)/shard_map/ppermute | solution.py:381
  61.2 20.1 %all-to-all-start = ((f32[4,128,256]{2,1,0:T(8,128)}), f32[4,128,256]{2,1,0:T(8,128)S(1)}, u32[]{:S(2)}, u32[]{:S(2)}) async-start(f32[4,128,256]{2,1,0:T(8,128)} %add_up.1), calls=%async_computation | async-start | bytes 1048576 | tf_op jit(solution)/shard_map/all_to_all | solution.py:387
  71.7 30.7 %copy-start.5 = (bf16[32,512]{1,0:T(8,128)(2,1)S(1)}, bf16[32,512]{1,0:T(8,128)(2,1)}, u32[]{:S(2)}) copy-start(bf16[32,512]{1,0:T(8,128)(2,1)} %residual.1) | copy-start | bytes 98308
  71.7 45.4 %copy-start.8 = (f32[512]{0:T(512)S(1)}, f32[512]{0:T(512)}, u32[]{:S(2)}) copy-start(f32[512]{0:T(512)} %param.15) | copy-start | bytes 6148
  71.7 8.4 %collective-permute-start.6 = (f32[128,256]{1,0:T(8,128)S(1)}, f32[128,256]{1,0:T(8,128)S(1)}, u32[]{:S(2)}, u32[]{:S(2)}) collective-permute-start(f32[128,256]{1,0:T(8,128)S(1)} %get-tuple-element.43), channel_id=1, source_target_pairs={{0,64},{64,128},{128,192},{192,256},{256,320},{320,384},{384,448},... | collective-permute-start | bytes 393224 | tf_op jit(solution)/shard_map/ppermute | solution.py:391
  73.7 7.7 %collective-permute-start.7 = (f32[128,256]{1,0:T(8,128)S(1)}, f32[128,256]{1,0:T(8,128)S(1)}, u32[]{:S(2)}, u32[]{:S(2)}) collective-permute-start(f32[128,256]{1,0:T(8,128)S(1)} %get-tuple-element.44), channel_id=1, source_target_pairs={{0,704},{64,0},{128,64},{192,128},{256,192},{320,256},{384,320},{4... | collective-permute-start | bytes 393224 | tf_op jit(solution)/shard_map/ppermute | solution.py:391
